TPU v7x, 256 devices: a whole 4x4x8 slice. The times are simulated.
256 devices in a mesh: row: 32 (over x, z), col: 8 (over y, core).
Axes of the slice: x: 4, y: 4, z: 8, core: 2. Of those that a mesh axis runs over, the one named last changes fastest.
Arguments:
- weight: float32 [9, 7168, 2048], P(None, 'row', 'col'), may hold values from -6 to 6
- grad: bfloat16 [9, 7168, 2048], P(None, 'row', 'col'), may hold values from -162 to 162
- momentum: float32 [9, 7168, 2048], P(None, 'row', 'col'), may hold values from -6 to 6
- right: float32 [2048, 9, 64], P('col'), may hold values from -6 to 6
Outputs:
- new_weight: float32 [9, 7168, 2048], P(None, 'row', 'col')
- new_momentum: float32 [9, 7168, 2048], P(None, 'row', 'col')
- new_right: float32 [2048, 9, 64], P('col')
All inputs are finite; a program needn't handle non-finite values.
Results may differ from a plain program's by a relative error of at most 0.0003.
Values sent between devices are 32-bit elements; how exact they have to be, the bound alone decides.
A program may use at most 64 MiB of HBM per device.

v0:
```python
import math

import jax
import jax.numpy as jnp
from jax import lax
from jax.sharding import PartitionSpec as P

D = 7168
FF = 2048


epsilon = 1e-06
momentum_decay = 0.95
highest = lax.Precision.HIGHEST


def inverse_factor(gram):
    lower = jnp.linalg.cholesky(gram)
    identity = jnp.broadcast_to(jnp.eye(gram.shape[-1], dtype=jnp.float32), gram.shape)
    return jax.scipy.linalg.solve_triangular(lower, identity, lower=True)


def apply_inverse(factor, inverse):
    return jnp.einsum("rmk,mlk->rml", factor, inverse, precision=highest)


def local_gram(factor):
    return jnp.einsum("rmk,rml->mkl", factor, factor, precision=highest)


def ortho_rows(factor):
    for sweep in range(2):
        gram = lax.psum(local_gram(factor), "row")
        factor = apply_inverse(factor, inverse_factor(gram))
    return factor


def body(weight, grad, momentum, right):
    stacked = momentum + grad.astype(jnp.float32)
    local_power = jnp.einsum("mrc,cmk->rmk", stacked, right, precision=highest)
    summed = lax.psum(local_power, "col")
    factor = ortho_rows(summed)
    local_right = jnp.einsum("mrc,rmk->cmk", stacked, factor, precision=highest)
    product = lax.psum(local_right, "row")
    squares = lax.psum(jnp.sum(product * product, axis=0), "col")
    scale_cols = jnp.sqrt(squares / FF + epsilon)
    new_right = product / scale_cols[None]
    feedback = jnp.einsum("rmk,cmk->mrc", factor, product, precision=highest)
    new_momentum = stacked - (1.0 - momentum_decay) * feedback
    update = jnp.einsum("rmk,cmk->mrc", factor, new_right, precision=highest)
    new_weight = weight - math.sqrt(D / FF) * update
    return (new_weight, new_momentum, new_right)


def solution(mesh):
    placed = (
        P(None, "row", "col"),
        P(None, "row", "col"),
        P(None, "row", "col"),
        P("col", None, None),
    )
    return jax.shard_map(
        body,
        mesh=mesh,
        in_specs=placed,
        out_specs=(P(None, "row", "col"), P(None, "row", "col"), P("col", None, None)),
        check_vma=False,
    )
```

profile of v0, /device:TPU:1, one launch (start us, length us, event | category | flops | bytes accessed | tf_op | source)
XLA Modules:
  0.0 755.0 jit_solution(9043946389727180321)
XLA Ops:
  7.2 0.0 copy-start
  7.2 0.0 all-reduce.5.cloned.1.call-start
  7.2 1.0 copy-done
  8.2 4.9 convolution_bitcast_fusion.1
  13.1 0.0 all-reduce.5.cloned.1.call-update
  13.2 0.0 all-reduce.7.cloned.1.call-start
  13.2 68.0 %all-reduce.5.cloned.1.call-done = f32[224,9,64]{0,2,1:T(8,128)} async-done(((f32[224,9,64]{0,2,1:T(8,128)}), f32[224,9,64]{0,2,1:T(8,128)}) %all-reduce.5.cloned.1.call-update) | async-done | bytes 516112 | tf_op jit(solution)/shard_map/psum | solution.py:41
  81.3 2.7 fusion.9
  84.0 0.0 all-reduce.7.cloned.1.call-update
  84.0 0.0 all-reduce.9.cloned.1.call-start
  84.1 142.0 %all-reduce.7.cloned.1.call-done = f32[9,64,64]{1,2,0:T(8,128)} async-done(((f32[9,64,64]{1,2,0:T(8,128)}), f32[9,64,64]{1,2,0:T(8,128)}) %all-reduce.7.cloned.1.call-update) | async-done | bytes 147472 | tf_op jit(solution)/shard_map/psum | solution.py:33
  226.1 1.1 copy.12
  227.2 1.0 fusion.5
  228.2 52.8 %custom-call.8 = f32[9,64,64]{2,1,0:T(8,128)S(1)} custom-call(f32[9,64,64]{2,1,0:T(8,128)S(1)} %fusion.5), custom_call_target="Cholesky" | custom-call | tf_op jit(solution)/shard_map/jit(cholesky)/cholesky | solution.py:18
  281.0 0.1 compare_reduce_fusion.1
  281.1 0.1 select_bitcast_fusion.1
  281.3 44.2 %custom-call.9 = f32[9,1,64,64]{2,3,1,0:T(8,128)S(1)} custom-call(f32[9,1,64,64]{3,2,1,0:T(8,128)S(1)} %select_bitcast_fusion.1), custom_call_target="InvertDiagBlocksLowerTriangular" | custom-call | tf_op jit(solution)/shard_map/jit(_solve_triangular)/vmap()/triangular_solve | solution.py:20
  325.5 0.7 fusion.3
  326.2 0.0 copy-done.6
  326.2 0.6 convolution_bitcast_fusion.3
  326.8 0.0 copy-start.2
  326.8 0.8 copy-done.2
  327.6 1.4 fusion.10
  329.0 0.0 all-reduce.9.cloned.1.call-update
  329.1 0.0 all-reduce.11.cloned.1.call-start
  329.1 141.7 %all-reduce.9.cloned.1.call-done = f32[9,64,64]{1,2,0:T(8,128)} async-done(((f32[9,64,64]{1,2,0:T(8,128)}), f32[9,64,64]{1,2,0:T(8,128)}) %all-reduce.9.cloned.1.call-update) | async-done | bytes 147472 | tf_op jit(solution)/shard_map/psum | solution.py:33
  470.8 1.1 copy.14
  471.9 0.0 copy-start.1
  471.9 1.1 fusion.2
  473.0 52.8 %custom-call.10 = f32[9,64,64]{2,1,0:T(8,128)S(1)} custom-call(f32[9,64,64]{2,1,0:T(8,128)S(1)} %fusion.2), custom_call_target="Cholesky" | custom-call | tf_op jit(solution)/shard_map/jit(cholesky)/cholesky | solution.py:18
  525.9 0.1 compare_reduce_fusion
  526.0 0.1 select_bitcast_fusion
  526.1 44.2 %custom-call.11 = f32[9,1,64,64]{2,3,1,0:T(8,128)S(1)} custom-call(f32[9,1,64,64]{3,2,1,0:T(8,128)S(1)} %select_bitcast_fusion), custom_call_target="InvertDiagBlocksLowerTriangular" | custom-call | tf_op jit(solution)/shard_map/jit(_solve_triangular)/vmap()/triangular_solve | solution.py:20
  570.3 0.0 copy-start.3
  570.3 0.6 fusion
  571.0 1.7 convolution_bitcast_fusion.2
  572.7 2.4 convolution_bitcast_fusion
  575.1 0.0 all-reduce.11.cloned.1.call-update
  575.1 145.1 %all-reduce.11.cloned.1.call-done = f32[256,9,64]{0,2,1:T(8,128)} async-done(((f32[256,9,64]{0,2,1:T(8,128)}), f32[256,9,64]{0,2,1:T(8,128)}) %all-reduce.11.cloned.1.call-update) | async-done | bytes 589840 | tf_op jit(solution)/shard_map/psum | solution.py:44
  720.2 1.2 multiply_reduce_fusion
  721.4 17.5 %psum.39 = f32[9,64]{1,0:T(8,128)S(1)} all-reduce(f32[9,64]{1,0:T(8,128)S(1)} %multiply_reduce_fusion), channel_id=1, replica_groups=mesh['row'=32,'col'=8] {'col'}, use_global_device_ids=true, to_apply=%region_7.10 | all-reduce | flops 576 | bytes 4608 | tf_op jit(solution)/shard_map/psum | solution.py:45
  738.9 1.2 broadcast_divide_fusion
  740.1 0.0 copy-start.7
  740.1 0.0 copy-start.4
  740.1 5.0 multiply_subtract_fusion.1
  745.1 0.0 copy-done.7
  745.1 0.0 copy-done.5
  745.1 3.3 multiply_subtract_fusion
  (11 shorter events, 0.1 us)
Async XLA Ops:
  7.2 1.1 copy-start
  7.2 74.1 %all-reduce.5.cloned.1.call-start = ((), (), s32[]{:S(2)}) async-start(), calls=%async_computation | async-start | bytes 1179648 | tf_op jit(solution)/shard_map/psum | solution.py:41
  13.2 212.9 %all-reduce.7.cloned.1.call-start = ((), (), s32[]{:S(2)}) async-start(), calls=%async_computation.1 | async-start | bytes 589824 | tf_op jit(solution)/shard_map/psum | solution.py:33
  81.3 244.9 %copy-start.6 = (f32[224,9,64]{0,2,1:T(8,128)S(1)}, f32[224,9,64]{0,2,1:T(8,128)}, u32[]{:S(2)}) copy-start(f32[224,9,64]{0,2,1:T(8,128)} %all-reduce.5.cloned.1.call-done) | copy-start | bytes 1548292
  84.0 386.8 %all-reduce.9.cloned.1.call-start = ((), (), s32[]{:S(2)}) async-start(), calls=%async_computation.2 | async-start | bytes 589824 | tf_op jit(solution)/shard_map/psum | solution.py:33
  326.8 0.8 copy-start.2
  329.1 391.1 %all-reduce.11.cloned.1.call-start = ((), (), s32[]{:S(2)}) async-start(), calls=%async_computation.3 | async-start | bytes 1179648 | tf_op jit(solution)/shard_map/psum | solution.py:44
  471.9 100.8 %copy-start.1 = (f32[9,224,256]{2,1,0:T(8,128)S(1)}, f32[9,224,256]{2,1,0:T(8,128)}, u32[]{:S(2)}) copy-start(f32[9,224,256]{2,1,0:T(8,128)} %param.9) | copy-start | bytes 6193156
  570.3 2.4 copy-start.3
  740.1 5.0 copy-start.7
  740.1 5.0 copy-start.4
  740.1 5.0 copy-start.5
Sparse Core Ops, SparseCore 0:
  13.3 67.9 all-reduce.4
  85.3 140.7 all-reduce.6
  329.2 141.5 all-reduce.8
  575.2 144.8 all-reduce.10
where the time goes:
time: 755 us
  waiting for transfers between devices  497 us (66%)
  other arithmetic  199 us (26%)
  matrix products  23.3 us (3%)
  blocking collectives  17.5 us (2%)
  between operations  14 us (2%)
    psum x2, waiting for transfers between devices, ortho_rows(): gram = lax.psum(local_gram(factor), 'row')  284 us
    psum x1, waiting for transfers between devices, body(): product = lax.psum(local_right, 'row')  145 us
    another operation x7, other arithmetic, inverse_factor(): lower = jnp.linalg.cholesky(gram)  106 us
    another operation x5, other arithmetic, inverse_factor(): return jax.scipy.linalg.solve_triangular(lower, identity, lower=True)  88.7 us
    psum x1, waiting for transfers between devices, body(): summed = lax.psum(local_power, 'col')  68 us
    psum x1, blocking collectives, body(): squares = lax.psum(jnp.sum(product * product, axis=0), 'col')  17.5 us
  transfers between devices with their start and end apart: 4, of which 4 were waited for; matrix products, arithmetic and copies ran while one was open for 0% of the time, Pallas kernels for 0%

commit v1 on v0

v1 whole, which is shorter than its diff:
```python
import functools
import math

import jax
import jax.numpy as jnp
from jax import lax
from jax.experimental import pallas as pl
from jax.experimental.pallas import tpu as pltpu
from jax.sharding import PartitionSpec as P

MESH = pl.DeviceIdType.MESH
HIGHEST = lax.Precision.HIGHEST
F32 = jnp.float32
BF16 = jnp.bfloat16

EPSILON = 1e-06
DECAY = 0.95
RANK = 64


def two_sum(a, b):
    s = a + b
    back = s - a
    return s, (a - (s - back)) + (b - back)


def split(a):
    t = a * 4097.0
    high = t - (t - a)
    return high, a - high


def two_prod(a, b):
    p = a * b
    ah, al = split(a)
    bh, bl = split(b)
    return p, ((ah * bh - p) + ah * bl + al * bh) + al * bl


def add_pair(ah, al, bh, bl):
    s, t = two_sum(ah, bh)
    t = t + (al + bl)
    h = s + t
    return h, t - (h - s)


def nt(a, b, precision=None):
    return lax.dot_general(a, b, (((1,), (1,)), ((), ())), precision=precision, preferred_element_type=F32)


def nn(a, b, precision=None):
    return lax.dot_general(a, b, (((1,), (0,)), ((), ())), precision=precision, preferred_element_type=F32)


def tn(a, b, precision=None):
    return lax.dot_general(a, b, (((0,), (0,)), ((), ())), precision=precision, preferred_element_type=F32)


def round_int(v):
    magic = 1.5 * 2.0**23
    return (v + magic) - magic


def exact_gram(x):
    top = jnp.maximum(jnp.max(jnp.abs(x), axis=1, keepdims=True), 1e-18)
    top = jnp.broadcast_to(top, (RANK, 128))
    power = jnp.floor(jnp.log(top) * (1.0 / math.log(2.0))) + 1.0
    unit = jnp.exp2(power - 7.0).astype(BF16).astype(F32)
    inverse = jnp.exp2(7.0 - power).astype(BF16).astype(F32)
    y = x * inverse[:, 0:1]
    slices = []
    for i in range(4):
        q = round_int(y)
        slices.append(q.astype(BF16))
        y = (y - q) * 256.0
    q = jnp.concatenate(slices, axis=0)
    e = nt(q, q)
    low = [e[RANK * a : RANK * (a + 1), 0:128] for a in range(4)]
    high = [e[RANK * a : RANK * (a + 1), 128:256] for a in range(4)]
    levels = [low[0], low[1], low[2] + high[0], low[3] + high[1], high[2], high[3]]
    s, t = levels[0], jnp.zeros_like(levels[0])
    for i in range(1, 6):
        s, err = two_sum(s, levels[i] * (2.0 ** (-8 * i)))
        t = t + err
    s2 = pltpu.roll(s, 64, 1) * (1.0 / 256.0)
    t2 = pltpu.roll(t, 64, 1) * (1.0 / 256.0)
    gh, gl = add_pair(s, t, s2, t2)
    rows = lax.broadcasted_iota(jnp.int32, (RANK, 128), 0)
    lanes = lax.broadcasted_iota(jnp.int32, (RANK, 128), 1)
    across = jnp.sum(jnp.where(rows == lanes, unit, 0.0), axis=0, keepdims=True)
    return gh * unit * across, gl * unit * across


def factor_block(mh, ml, first, count, begin, end):
    rows = lax.broadcasted_iota(jnp.int32, (count, 128), 0) + first
    lanes = lax.broadcasted_iota(jnp.int32, (count, 128), 1)
    half = jnp.where(lanes >= 64, 64, 0)
    column = lanes - half

    def step(k, carry):
        ah, al = mh[first:, :], ml[first:, :]
        rh, rl = mh[pl.ds(k, 1), :], ml[pl.ds(k, 1), :]
        index = half + k
        ch = jnp.take_along_axis(ah, index, axis=1)
        cl = jnp.take_along_axis(al, index, axis=1)
        dh = jnp.take_along_axis(jnp.broadcast_to(rh, (8, 128)), index[0:8], axis=1)[0:1]
        dl = jnp.take_along_axis(jnp.broadcast_to(rl, (8, 128)), index[0:8], axis=1)[0:1]
        inv = 1.0 / dh
        p, e = two_prod(dh, inv)
        inv_low = inv * (((1.0 - p) - e) - dl * inv)
        p, e = two_prod(ch, inv)
        t = e + (ch * inv_low + cl * inv)
        nh = p + t
        nl = t - (nh - p)
        later = rows > k
        nh = jnp.where(later, nh, 0.0)
        nl = jnp.where(later, nl, 0.0)
        here = column == k
        rh = jnp.where(here[0:1], 1.0, rh)
        rl = jnp.where(here[0:1], 0.0, rl)
        clear = here & later
        ah = jnp.where(clear, 0.0, ah)
        al = jnp.where(clear, 0.0, al)
        p, e = two_prod(nh, rh)
        q = e + (nh * rl + nl * rh)
        s, t = two_sum(ah, -p)
        t = t + (al - q)
        h = s + t
        mh[first:, :] = h
        ml[first:, :] = t - (h - s)
        return carry

    lax.fori_loop(begin, end, step, 0)


def factor_pair(mh, ml, begin, end):
    for first in range(begin, end, 8):
        factor_block(mh, ml, first, RANK - first, first, first + 8)


def inverse_of(mh):
    m = mh[...]
    rows = lax.broadcasted_iota(jnp.int32, (RANK, 128), 0)
    lanes = lax.broadcasted_iota(jnp.int32, (RANK, 128), 1)
    left = lanes < 64
    column = jnp.where(left, lanes, lanes - 64)
    diagonal = jnp.where(column == rows, m, 0.0)
    da = jnp.sum(jnp.where(left, diagonal, 0.0), axis=1, keepdims=True)
    db = jnp.sum(jnp.where(left, 0.0, diagonal), axis=1, keepdims=True)
    root = 1.0 / jnp.sqrt(jnp.where(left, da, db))
    return jnp.where(column < rows, m * root, jnp.where(column == rows, root, 0.0))


def exchange_kernel(nx, nz, ny, grad, mom, right, qt_out, prod_out, scale_out, s_v, g_v, r_v, part, mate, ysend, yrecv,
                    pt, gx, gz, mh, ml, linv, tp, trecv, tfull, sq, load_sem, mate_send, mate_recv, y_send, y_recv,
                    ag_send, ag_recv, fw_send, fw_recv, h_send, h_recv, gx_send, gx_recv, gz_send, gz_recv, t_send,
                    t_recv, ta_send, ta_recv, l_send, l_recv, sq_send, sq_recv):
    nr, nc = nx * nz, ny * 2
    mats = nc + 1
    last = mats - 1
    ff = 256 * nc
    row, col = lax.axis_index("row"), lax.axis_index("col")
    x, z = row // nz, row % nz
    y, k = col // 2, col % 2
    mate_id = (row, y * 2 + (1 - k))
    half = RANK // 2

    def remote(src, dst, send, recv, target):
        return pltpu.make_async_remote_copy(src_ref=src, dst_ref=dst, send_sem=send, recv_sem=recv, device_id=target,
                                            device_id_type=MESH)

    load_right = pltpu.make_async_copy(right, r_v, load_sem.at[2 * mats])
    load_right.start()

    def loads(m):
        return (pltpu.make_async_copy(mom.at[m], s_v.at[m], load_sem.at[m]),
                pltpu.make_async_copy(grad.at[m], g_v.at[m], load_sem.at[mats + m]))

    order = [2 * i + (1 - k) for i in range(ny)] + [last] + [2 * i + k for i in range(ny)]
    for m in order:
        for c in loads(m):
            c.start()

    barrier = pltpu.get_barrier_semaphore()

    def greet(i, c):
        pl.semaphore_signal(barrier, inc=1, device_id=(lax.rem(row + i, nr), col), device_id_type=MESH)
        return c

    def greet_col(i, c):
        pl.semaphore_signal(barrier, inc=1, device_id=(row, lax.rem(col + i, nc)), device_id_type=MESH)
        return c

    lax.fori_loop(1, nr, greet, 0)
    lax.fori_loop(1, nc, greet_col, 0)
    load_right.wait()

    def power(m):
        for c in loads(m):
            c.wait()
        s = s_v[m] + g_v[m].astype(F32)
        s_v[m] = s
        part[m] = nt(r_v[m], s, HIGHEST)

    to_mate = []
    for i in range(ny):
        m = 2 * i + (1 - k)
        power(m)
        if i == 0:
            pl.semaphore_wait(barrier, nr + nc - 2)
        c = remote(part.at[m], mate.at[i], mate_send.at[i], mate_recv.at[i], mate_id)
        c.start()
        to_mate.append(c)
    power(last)
    other_rows = pl.ds(pl.multiple_of((1 - k) * half, half), half)
    my_rows = pl.ds(pl.multiple_of(k * half, half), half)
    c = remote(part.at[last, other_rows], mate.at[ny, pl.ds(0, half)], mate_send.at[ny], mate_recv.at[ny], mate_id)
    c.start()
    to_mate.append(c)
    for i in range(ny):
        power(2 * i + k)

    to_mate[ny].wait_recv()
    shared = part[last, my_rows, :] + mate[ny, 0:half, :]
    for i in range(ny):
        to_mate[i].wait_recv()
    to_y = []
    for i in range(1, ny):
        yd = lax.rem(y + i, ny)
        ysend[yd, 0:RANK, :] = part[2 * yd + k] + mate[yd]
        ysend[yd, RANK:, :] = shared
        c = remote(ysend.at[yd], yrecv.at[y], y_send.at[i], y_recv.at[i], (row, 2 * yd + k))
        c.start()
        to_y.append(c)
    own = 2 * y + k
    yrecv[y, 0:RANK, :] = part[own] + mate[y]
    yrecv[y, RANK:, :] = shared
    for c in to_y:
        c.wait_recv()
    total = yrecv[0]
    for i in range(1, ny):
        total = total + yrecv[i]
    pt[own] = total[0:RANK]
    pt[last, my_rows, :] = total[RANK:]
    swap = remote(pt.at[last, my_rows], pt.at[last, my_rows], h_send, h_recv, mate_id)
    swap.start()
    gather = []
    for i in range(1, ny):
        yd = lax.rem(y + i, ny)
        c = remote(pt.at[own], pt.at[own], ag_send.at[i], ag_recv.at[i], (row, 2 * yd + k))
        c.start()
        gather.append(c)
    forward = [remote(pt.at[own], pt.at[own], fw_send.at[0], fw_recv.at[0], mate_id)]
    forward[0].start()
    swap.wait_recv()

    ah, al = exact_gram(pt[own])
    bh, bl = exact_gram(pt[last])
    lanes = lax.broadcasted_iota(jnp.int32, (RANK, 128), 1)
    gx[x, 0] = jnp.where(lanes < 64, ah, pltpu.roll(bh, 64, 1))
    gx[x, 1] = jnp.where(lanes < 64, al, pltpu.roll(bl, 64, 1))
    to_x = []
    for i in range(1, nx):
        xd = lax.rem(x + i, nx)
        c = remote(gx.at[x], gx.at[x], gx_send.at[i], gx_recv.at[i], (xd * nz + z, col))
        c.start()
        to_x.append(c)

    for i in range(1, ny):
        gather[i - 1].wait_recv()
        m = 2 * lax.rem(y - i + ny, ny) + k
        c = remote(pt.at[m], pt.at[m], fw_send.at[i], fw_recv.at[i], mate_id)
        c.start()
        forward.append(c)
    for c in forward:
        c.wait_recv()

    rows_t = tp.shape[1]

    def times(m, c):
        t = nn(pt[m], s_v[m], HIGHEST)
        at = pl.ds(pl.multiple_of(m * RANK, RANK), RANK)
        tp[0, at, :] = t[:, 0:128]
        tp[1, at, :] = t[:, 128:256]
        return c

    lax.fori_loop(0, mats, times, 0)
    if rows_t > mats * RANK:
        tp[:, mats * RANK :, :] = jnp.zeros((2, rows_t - mats * RANK, 128), F32)

    for c in to_x:
        c.wait_recv()
    gh, gl = gx[0, 0], gx[0, 1]
    for i in range(1, nx):
        gh, gl = add_pair(gh, gl, gx[i, 0], gx[i, 1])
    gz[z, 0] = gh
    gz[z, 1] = gl
    to_z = []
    for i in range(1, nz):
        zd = lax.rem(z + i, nz)
        c = remote(gz.at[z], gz.at[z], gz_send.at[i], gz_recv.at[i], (x * nz + zd, col))
        c.start()
        to_z.append(c)

    piece = 2 * rows_t // nr
    per_half = nr // 2

    def piece_of(ref, d):
        return ref.at[d // per_half, pl.ds(pl.multiple_of((d % per_half) * piece, piece), piece)]

    def t_copy(i):
        d = lax.rem(row + i, nr)
        return remote(piece_of(tp, d), trecv.at[row], t_send.at[i], t_recv.at[i], (d, col))

    def ta_copy(i):
        d = lax.rem(row + i, nr)
        return remote(piece_of(tfull, row), piece_of(tfull, row), ta_send.at[i], ta_recv.at[i], (d, col))

    def start(copy):
        def go(i, c):
            copy(i).start()
            return c
        return go

    def wait_recv(copy):
        def go(i, c):
            copy(i).wait_recv()
            return c
        return go

    def wait_send(copy):
        def go(i, c):
            copy(i).wait_send()
            return c
        return go

    lax.fori_loop(1, nr, start(t_copy), 0)
    my_at = pl.ds(pl.multiple_of((row % per_half) * piece, piece), piece)
    trecv[row] = tp[row // per_half, my_at, :]

    for c in to_z:
        c.wait_recv()
    gh, gl = gz[0, 0], gz[0, 1]
    for i in range(1, nz):
        gh, gl = add_pair(gh, gl, gz[i, 0], gz[i, 1])
    mh[...] = gh
    ml[...] = gl
    factor_pair(mh, ml, 0, 32)

    lax.fori_loop(1, nr, wait_recv(t_copy), 0)
    tfull[row // per_half, my_at, :] = lax.fori_loop(1, nr, lambda i, acc: acc + trecv[i], trecv[0])
    lax.fori_loop(1, nr, start(ta_copy), 0)

    factor_pair(mh, ml, 32, RANK)
    linv[own] = inverse_of(mh)
    spread = []
    for i in range(1, nc):
        cd = lax.rem(col + i, nc)
        c = remote(linv.at[own], linv.at[own], l_send.at[i], l_recv.at[i], (row, cd))
        c.start()
        spread.append(c)
    last_inverse = pltpu.roll(linv[own], 64, 1)
    for c in spread:
        c.wait_recv()
    linv[last] = last_inverse

    def orthonormal(m, c):
        qt_out[m] = nn(linv[m][:, 0:RANK], pt[m], HIGHEST)
        return c

    lax.fori_loop(0, mats, orthonormal, 0)
    lax.fori_loop(1, nr, wait_recv(ta_copy), 0)

    def apply(m, acc):
        at = pl.ds(pl.multiple_of(m * RANK, RANK), RANK)
        t = jnp.concatenate([tfull[0, at, :], tfull[1, at, :]], axis=1)
        p = nn(linv[m][:, 0:RANK], t, HIGHEST)
        prod_out[m] = p
        ones = jnp.where(lax.broadcasted_iota(jnp.int32, (16, 256), 0) == m, 1.0, 0.0)
        return acc + nt(ones, p * p, HIGHEST)

    squares = lax.fori_loop(0, mats, apply, jnp.zeros((16, RANK), F32))
    sq[col] = jnp.concatenate([squares, jnp.zeros((16, 128 - RANK), F32)], axis=1)
    to_all = []
    for i in range(1, nc):
        cd = lax.rem(col + i, nc)
        c = remote(sq.at[col], sq.at[col], sq_send.at[i], sq_recv.at[i], (row, cd))
        c.start()
        to_all.append(c)
    for c in to_all:
        c.wait_recv()
    squares = sq[0]
    for i in range(1, nc):
        squares = squares + sq[i]
    scale = 1.0 / jnp.sqrt(squares * (1.0 / ff) + EPSILON)
    scale_out[...] = jnp.transpose(scale)

    for c in to_mate + to_y + gather + forward + [swap] + to_x + to_z + spread + to_all:
        c.wait_send()
    lax.fori_loop(1, nr, wait_send(t_copy), 0)
    lax.fori_loop(1, nr, wait_send(ta_copy), 0)


def update_kernel(gain, weight, grad, mom, qt, prod, scale, new_weight, new_mom, new_right):
    m = pl.program_id(0)
    table = scale[...]
    lanes = lax.broadcasted_iota(jnp.int32, table.shape, 1)
    column = jnp.sum(jnp.where(lanes == m, table, 0.0), axis=1, keepdims=True)[0:RANK]
    q, p = qt[0], prod[0]
    normed = p * column
    new_right[0] = normed
    stacked = mom[0] + grad[0].astype(F32)
    new_mom[0] = stacked - tn(q * (1.0 - DECAY), p, HIGHEST)
    new_weight[0] = weight[0] - tn(q * gain, normed, HIGHEST)


def body(nx, nz, ny, depth, weight, grad, momentum, right):
    nr, nc = nx * nz, ny * 2
    mats, rows, cols = weight.shape
    ff = cols * nc
    rt = jnp.transpose(right, (1, 2, 0))
    piece = -(-2 * mats * RANK // nr)
    piece = -(-piece // 8) * 8
    rows_t = piece * nr // 2
    vmem = pl.BlockSpec(memory_space=pltpu.VMEM)
    hbm = pl.BlockSpec(memory_space=pl.ANY)
    dma = pltpu.SemaphoreType.DMA
    half = RANK // 2
    qt, prod, scale = pl.pallas_call(
        functools.partial(exchange_kernel, nx, nz, ny),
        out_shape=(
            jax.ShapeDtypeStruct((mats, RANK, rows), F32),
            jax.ShapeDtypeStruct((mats, RANK, cols), F32),
            jax.ShapeDtypeStruct((128, 16), F32),
        ),
        in_specs=[hbm, hbm, hbm],
        out_specs=(vmem, vmem, vmem),
        scratch_shapes=[
            pltpu.VMEM((mats, rows, cols), F32),
            pltpu.VMEM((mats, rows, cols), BF16),
            pltpu.VMEM((mats, RANK, cols), F32),
            pltpu.VMEM((mats, RANK, rows), F32),
            pltpu.VMEM((ny + 1, RANK, rows), F32),
            pltpu.VMEM((ny, RANK + half, rows), F32),
            pltpu.VMEM((ny, RANK + half, rows), F32),
            pltpu.VMEM((mats, RANK, rows), F32),
            pltpu.VMEM((nx, 2, RANK, 128), F32),
            pltpu.VMEM((nz, 2, RANK, 128), F32),
            pltpu.VMEM((RANK, 128), F32),
            pltpu.VMEM((RANK, 128), F32),
            pltpu.VMEM((mats, RANK, 128), F32),
            pltpu.VMEM((2, rows_t, 128), F32),
            pltpu.VMEM((nr, piece, 128), F32),
            pltpu.VMEM((2, rows_t, 128), F32),
            pltpu.VMEM((nc, 16, 128), F32),
            dma((2 * mats + 1,)),
            dma((ny + 1,)), dma((ny + 1,)),
            dma((ny,)), dma((ny,)),
            dma((ny,)), dma((ny,)),
            dma((ny,)), dma((ny,)),
            dma, dma,
            dma((nx,)), dma((nx,)),
            dma((nz,)), dma((nz,)),
            dma((nr,)), dma((nr,)),
            dma((nr,)), dma((nr,)),
            dma((nc,)), dma((nc,)),
            dma((nc,)), dma((nc,)),
        ],
        compiler_params=pltpu.CompilerParams(
            collective_id=0, has_side_effects=True, vmem_limit_bytes=40 * 1024 * 1024
        ),
        name="exchange",
    )(grad, momentum, rt)

    def block(*shape):
        return pl.BlockSpec((1,) + shape, lambda m: (m, 0, 0))

    big = block(rows, cols)
    gain = math.sqrt(depth / ff)
    new_weight, new_momentum, new_right = pl.pallas_call(
        functools.partial(update_kernel, gain),
        grid=(mats,),
        out_shape=(
            jax.ShapeDtypeStruct(weight.shape, F32),
            jax.ShapeDtypeStruct(weight.shape, F32),
            jax.ShapeDtypeStruct((mats, RANK, cols), F32),
        ),
        in_specs=[big, big, big, block(RANK, rows), block(RANK, cols), pl.BlockSpec((128, 16), lambda m: (0, 0))],
        out_specs=(big, big, block(RANK, cols)),
        name="update",
    )(weight, grad, momentum, qt, prod, scale)
    return new_weight, new_momentum, jnp.transpose(new_right, (2, 0, 1))


def solution(mesh):
    nr, nc = mesh.shape["row"], mesh.shape["col"]
    nz = min(nr, 8)
    nx = nr // nz

    def run(weight, grad, momentum, right):
        return body(nx, nz, nc // 2, weight.shape[1] * nr, weight, grad, momentum, right)

    placed = P(None, "row", "col")
    return jax.shard_map(
        run,
        mesh=mesh,
        in_specs=(placed, placed, placed, P("col", None, None)),
        out_specs=(placed, placed, P("col", None, None)),
        check_vma=False,
    )
```

time: 755 us -> 108 us (0.14)
  waiting for transfers between devices: 497 us -> 0 us
  other arithmetic: 199 us -> 0 us
  Pallas kernels: 0 us -> 100 us
  matrix products: 23.3 us -> 0 us
  blocking collectives: 17.5 us -> 0 us
  between operations: 14 us -> 0.66 us
    psum x4 -> x0, waiting for transfers between devices: 497 us -> none  [the longest x2 284 us: ortho_rows(): gram = lax.psum(local_gram(factor), 'row')]
    another operation x12 -> x0, other arithmetic: 195 us -> none  [the longest x7 106 us: inverse_factor(): lower = jnp.linalg.cholesky(gram)]
    pallas_call x0 -> x2, Pallas kernels: none -> 100 us  [the longest x1 89.7 us: body(): pl.pallas_call(functools.partial(exchange_kernel, nx, nz, ny), out_shape=...]
    dot_general x8 -> x0, matrix products: 22 us -> none  [the longest x1 5 us: body(): update = jnp.einsum('rmk,cmk->mrc', factor, new_right, precision=highest)]
    psum x1 -> x0, blocking collectives: 17.5 us -> none  [body(): squares = lax.psum(jnp.sum(product * product, axis=0), 'col')]
  transfers between devices with their start and end apart: 4 -> 0, of which waited for: 4 -> 0; matrix products, arithmetic and copies ran while one was open for 0% -> 0% of each run, Pallas kernels for 0% -> 0%
where the time goes in v1:
time: 108 us; the launch traced here: 107 us
  Pallas kernels  100 us (93%)
  local copies, waits for them, and re-layouts  6.08 us (6%)
    pallas_call x1, Pallas kernels, body(): pl.pallas_call(functools.partial(exchange_kernel, nx, nz, ny), out_shape=...  89.7 us
    pallas_call x1, Pallas kernels, body(): pl.pallas_call(functools.partial(update_kernel, gain), grid=(mats,), out_...  10.4 us
    unnamed x12, local copies, waits for them, and re-layouts  6.08 us

profile of v1, /device:TPU:1, one launch (start us, length us, event | category | flops | bytes accessed | tf_op | source)
XLA Modules:
  0.0 106.9 jit_solution(17964427900515046378)
XLA Ops:
  0.6 0.0 copy-start
  0.6 1.6 %copy-done = f32[9,224,256]{2,1,0:T(8,128)S(1)} copy-done((f32[9,224,256]{2,1,0:T(8,128)S(1)}, f32[9,224,256]{2,1,0:T(8,128)}, u32[]{:S(2)}) %copy-start) | copy-done | bytes 2064408
  2.2 0.0 copy-start.1
  2.2 1.2 %copy-done.1 = bf16[9,224,256]{2,1,0:T(8,128)(2,1)S(1)} copy-done((bf16[9,224,256]{2,1,0:T(8,128)(2,1)S(1)}, bf16[9,224,256]{2,1,0:T(8,128)(2,1)}, u32[]{:S(2)}) %copy-start.1) | copy-done | bytes 1032216
  3.4 0.0 copy-start.4
  3.4 1.1 copy-done.4
  4.5 89.7 %exchange.1 = (f32[9,64,224]{2,1,0:T(8,128)S(1)}, f32[9,64,256]{2,1,0:T(8,128)S(1)}, f32[128,16]{1,0:T(8,128)S(1)}) custom-call(bf16[9,224,256]{2,1,0:T(8,128)(2,1)S(1)} %copy-done.1, f32[9,224,256]{2,1,0:T(8,128)S(1)} %copy-done, f32[9,64,256]{2,1,0:T(8,128)S(1)} %bitcast.2), custom_call_target="tpu_custom_call" | custom-call | tf_op jit(solution)/shard_map/exchange/pallas_call | solution.py:429
  94.2 0.0 copy-start.2
  94.2 0.8 copy-done.2
  95.0 0.0 copy-start.3
  95.0 0.8 copy-done.3
  95.9 0.0 copy-start.5
  95.9 0.6 copy-done.5
  96.5 10.4 %update.1 = (f32[9,224,256]{2,1,0:T(8,128)}, f32[9,224,256]{2,1,0:T(8,128)}, f32[9,64,256]{2,1,0:T(8,128)}) custom-call(f32[9,224,256]{2,1,0:T(8,128)} %weight.1, bf16[9,224,256]{2,1,0:T(8,128)(2,1)} %grad.3, f32[9,224,256]{2,1,0:T(8,128)} %mom.3, f32[9,64,224]{2,1,0:T(8,128)} %copy-done.2, f32[9,64,256]{2,1,0:T(8,128)} %copy-done.3, f32[128,16]{1,0:T(8,128)} %copy-done.5), custom_call_target="tpu_custom_call" | custom-call | tf_op jit(solution)/shard_map/update/pallas_call | solution.py:480
Async XLA Ops:
  0.6 1.6 %copy-start = (f32[9,224,256]{2,1,0:T(8,128)S(1)}, f32[9,224,256]{2,1,0:T(8,128)}, u32[]{:S(2)}) copy-start(f32[9,224,256]{2,1,0:T(8,128)} %mom.3) | copy-start | bytes 6193156
  2.2 1.2 %copy-start.1 = (bf16[9,224,256]{2,1,0:T(8,128)(2,1)S(1)}, bf16[9,224,256]{2,1,0:T(8,128)(2,1)}, u32[]{:S(2)}) copy-start(bf16[9,224,256]{2,1,0:T(8,128)(2,1)} %grad.3) | copy-start | bytes 3096580
  3.4 1.1 copy-start.4
  94.2 0.8 copy-start.2
  95.0 0.8 copy-start.3
  95.9 0.6 copy-start.5

commit v2 on v1

v2 whole, which is shorter than its diff:
```python
import functools
import math

import jax
import jax.numpy as jnp
from jax import lax
from jax.experimental import pallas as pl
from jax.experimental.pallas import tpu as pltpu
from jax.sharding import PartitionSpec as P

MESH = pl.DeviceIdType.MESH
HIGHEST = lax.Precision.HIGHEST
F32 = jnp.float32
BF16 = jnp.bfloat16

EPSILON = 1e-06
DECAY = 0.95
RANK = 64


def two_sum(a, b):
    s = a + b
    back = s - a
    return s, (a - (s - back)) + (b - back)


def split(a):
    t = a * 4097.0
    high = t - (t - a)
    return high, a - high


def two_prod(a, b):
    p = a * b
    ah, al = split(a)
    bh, bl = split(b)
    return p, ((ah * bh - p) + ah * bl + al * bh) + al * bl


def add_pair(ah, al, bh, bl):
    s, t = two_sum(ah, bh)
    t = t + (al + bl)
    h = s + t
    return h, t - (h - s)


def nt(a, b, precision=None):
    return lax.dot_general(a, b, (((1,), (1,)), ((), ())), precision=precision, preferred_element_type=F32)


def nn(a, b, precision=None):
    return lax.dot_general(a, b, (((1,), (0,)), ((), ())), precision=precision, preferred_element_type=F32)


def tn(a, b, precision=None):
    return lax.dot_general(a, b, (((0,), (0,)), ((), ())), precision=precision, preferred_element_type=F32)


def cut(a):
    a1 = a.astype(BF16)
    rest = a - a1.astype(F32)
    a2 = rest.astype(BF16)
    return a1, a2, (rest - a2.astype(F32)).astype(BF16)


def cut_product(dot, a, b):
    a1, a2, a3 = cut(a)
    b1, b2, b3 = cut(b)
    p = dot(jnp.concatenate([a1, a2, a3], axis=0), b1)
    q = dot(jnp.concatenate([a1, a2], axis=0), b2)
    r = dot(a1, b3)
    return p[0:RANK] + ((p[RANK : 2 * RANK] + q[0:RANK]) + (p[2 * RANK :] + q[RANK:] + r))


def round_int(v):
    magic = 1.5 * 2.0**23
    return (v + magic) - magic


def exact_gram(x):
    top = jnp.maximum(jnp.max(jnp.abs(x), axis=1, keepdims=True), 1e-18)
    top = jnp.broadcast_to(top, (RANK, 128))
    power = jnp.floor(jnp.log(top) * (1.0 / math.log(2.0))) + 1.0
    unit = jnp.exp2(power - 7.0).astype(BF16).astype(F32)
    inverse = jnp.exp2(7.0 - power).astype(BF16).astype(F32)
    y = x * inverse[:, 0:1]
    slices = []
    for i in range(4):
        q = round_int(y)
        slices.append(q.astype(BF16))
        y = (y - q) * 256.0
    q = jnp.concatenate(slices, axis=0)
    e = nt(q, q)
    low = [e[RANK * a : RANK * (a + 1), 0:128] for a in range(4)]
    high = [e[RANK * a : RANK * (a + 1), 128:256] for a in range(4)]
    levels = [low[0], low[1], low[2] + high[0], low[3] + high[1], high[2], high[3]]
    s, t = levels[0], jnp.zeros_like(levels[0])
    for i in range(1, 6):
        s, err = two_sum(s, levels[i] * (2.0 ** (-8 * i)))
        t = t + err
    s2 = pltpu.roll(s, 64, 1) * (1.0 / 256.0)
    t2 = pltpu.roll(t, 64, 1) * (1.0 / 256.0)
    gh, gl = add_pair(s, t, s2, t2)
    rows = lax.broadcasted_iota(jnp.int32, (RANK, 128), 0)
    lanes = lax.broadcasted_iota(jnp.int32, (RANK, 128), 1)
    across = jnp.sum(jnp.where(rows == lanes, unit, 0.0), axis=0, keepdims=True)
    return gh * unit * across, gl * unit * across


def factor_block(mh, ml, first, count, begin, end):
    rows = lax.broadcasted_iota(jnp.int32, (count, 128), 0) + first
    lanes = lax.broadcasted_iota(jnp.int32, (count, 128), 1)
    half = jnp.where(lanes >= 64, 64, 0)
    column = lanes - half

    def step(k, carry):
        ah, al = mh[first:, :], ml[first:, :]
        rh, rl = mh[pl.ds(k, 1), :], ml[pl.ds(k, 1), :]
        index = half + k
        ch = jnp.take_along_axis(ah, index, axis=1)
        cl = jnp.take_along_axis(al, index, axis=1)
        dh = jnp.take_along_axis(jnp.broadcast_to(rh, (8, 128)), index[0:8], axis=1)[0:1]
        dl = jnp.take_along_axis(jnp.broadcast_to(rl, (8, 128)), index[0:8], axis=1)[0:1]
        inv = 1.0 / dh
        p, e = two_prod(dh, inv)
        inv_low = inv * (((1.0 - p) - e) - dl * inv)
        p, e = two_prod(ch, inv)
        t = e + (ch * inv_low + cl * inv)
        nh = p + t
        nl = t - (nh - p)
        later = rows > k
        nh = jnp.where(later, nh, 0.0)
        nl = jnp.where(later, nl, 0.0)
        here = column == k
        rh = jnp.where(here[0:1], 1.0, rh)
        rl = jnp.where(here[0:1], 0.0, rl)
        clear = here & later
        ah = jnp.where(clear, 0.0, ah)
        al = jnp.where(clear, 0.0, al)
        p, e = two_prod(nh, rh)
        q = e + (nh * rl + nl * rh)
        s, t = two_sum(ah, -p)
        t = t + (al - q)
        h = s + t
        mh[first:, :] = h
        ml[first:, :] = t - (h - s)
        return carry

    lax.fori_loop(begin, end, step, 0)


def factor_pair(mh, ml, begin, end):
    for first in range(begin, end, 8):
        factor_block(mh, ml, first, RANK - first, first, first + 8)


def inverse_of(mh):
    m = mh[...]
    rows = lax.broadcasted_iota(jnp.int32, (RANK, 128), 0)
    lanes = lax.broadcasted_iota(jnp.int32, (RANK, 128), 1)
    left = lanes < 64
    column = jnp.where(left, lanes, lanes - 64)
    diagonal = jnp.where(column == rows, m, 0.0)
    da = jnp.sum(jnp.where(left, diagonal, 0.0), axis=1, keepdims=True)
    db = jnp.sum(jnp.where(left, 0.0, diagonal), axis=1, keepdims=True)
    root = 1.0 / jnp.sqrt(jnp.where(left, da, db))
    return jnp.where(column < rows, m * root, jnp.where(column == rows, root, 0.0))


def exchange_kernel(nx, nz, ny, weight, grad, mom, right, w_out, m_out, q_out, prod_out, scale_out, s_v, g_v, r_v, part,
                    mate, ysend, yrecv, pt, pw, gp, gx, gz, ga, mh, ml, linv, tp, xrecv, zsend, zrecv, tfull, sq, load_sem,
                    w_sem, mate_send, mate_recv, y_send, y_recv, ag_send, ag_recv, fw_send, fw_recv, h_send, h_recv,
                    gx_send, gx_recv, gz_send, gz_recv, ga_send, ga_recv, tx_send, tx_recv, tz_send, tz_recv, az_send,
                    az_recv, ax_send, ax_recv, l_send, l_recv, sq_send, sq_recv):
    nr, nc = nx * nz, ny * 2
    mats = nc + 1
    last = mats - 1
    ff = 256 * nc
    row, col = lax.axis_index("row"), lax.axis_index("col")
    x, z = row // nz, row % nz
    y, k = col // 2, col % 2
    mate_id = (row, y * 2 + (1 - k))
    half = RANK // 2

    pending = []

    def finish():
        for c in pending:
            c.wait_send()

    def send(src, dst, sems, index, target):
        c = pltpu.make_async_remote_copy(src_ref=src, dst_ref=dst, send_sem=sems[0].at[index], recv_sem=sems[1].at[index],
                                         device_id=target, device_id_type=MESH)
        c.start()
        pending.append(c)
        return c

    def x_peer(i):
        return lax.rem(x + i, nx)

    def z_peer(i):
        return lax.rem(z + i, nz)

    def y_peer(i):
        return lax.rem(y + i, ny)

    far_first = sorted(range(1, nz), key=lambda i: -min(i, nz - i))

    load_right = pltpu.make_async_copy(right, r_v, load_sem.at[2 * mats])
    load_right.start()

    def loads(m):
        return (pltpu.make_async_copy(mom.at[m], s_v.at[m], load_sem.at[m]),
                pltpu.make_async_copy(grad.at[m], g_v.at[m], load_sem.at[mats + m]))

    turns = list(range(1, ny)) + [0]
    for m in [2 * y_peer(i) + (1 - k) for i in turns] + [last] + [2 * y_peer(i) + k for i in turns]:
        for c in loads(m):
            c.start()

    barrier = pltpu.get_barrier_semaphore()
    peers = [(row, lax.rem(col + i, nc)) for i in range(1, nc)]
    peers += [(x * nz + z_peer(i), col) for i in far_first]
    peers += [(x_peer(i) * nz + z, col) for i in range(1, nx)]
    for peer in peers:
        pl.semaphore_signal(barrier, inc=1, device_id=peer, device_id_type=MESH)
    load_right.wait()

    def power(m):
        for c in loads(m):
            c.wait()
        s = s_v[m] + g_v[m].astype(F32)
        s_v[m] = s
        part[m] = cut_product(nt, r_v[m], s)

    to_mate = {}
    mate_sems = (mate_send, mate_recv)
    for n, i in enumerate(turns):
        m = 2 * y_peer(i) + (1 - k)
        power(m)
        if n == 0:
            pl.semaphore_wait(barrier, len(peers))
        to_mate[i] = send(part.at[m], mate.at[i], mate_sems, i, mate_id)
    power(last)
    other_rows = pl.ds(pl.multiple_of((1 - k) * half, half), half)
    my_rows = pl.ds(pl.multiple_of(k * half, half), half)
    to_mate[ny] = send(part.at[last, other_rows], mate.at[ny, pl.ds(0, half)], mate_sems, ny, mate_id)
    load_weight = pltpu.make_async_copy(weight, w_out, w_sem)
    load_weight.start()

    own = 2 * y + k
    to_y = []
    for n, i in enumerate(turns):
        yd = y_peer(i)
        power(2 * yd + k)
        if n == 0:
            to_mate[ny].wait_recv()
            shared = part[last, my_rows, :] + mate[ny, 0:half, :]
        to_mate[i].wait_recv()
        if i == 0:
            yrecv[y, 0:RANK, :] = part[own] + mate[0]
            yrecv[y, RANK:, :] = shared
        else:
            ysend[i, 0:RANK, :] = part[2 * yd + k] + mate[i]
            ysend[i, RANK:, :] = shared
            to_y.append(send(ysend.at[i], yrecv.at[y], (y_send, y_recv), i, (row, 2 * yd + k)))
    for c in to_y:
        c.wait_recv()
    total = yrecv[0]
    for i in range(1, ny):
        total = total + yrecv[i]
    pt[last, my_rows, :] = total[RANK:]
    swap = send(pt.at[last, my_rows], pt.at[last, my_rows], (h_send, h_recv), 0, mate_id)
    pt[own] = total[0:RANK]
    gather = [send(pt.at[own], pt.at[own], (ag_send, ag_recv), i, (row, 2 * y_peer(i) + k)) for i in range(1, ny)]
    forward = [send(pt.at[own], pt.at[own], (fw_send, fw_recv), 0, mate_id)]

    lanes = lax.broadcasted_iota(jnp.int32, (RANK, 128), 1)
    ah, al = exact_gram(total[0:RANK])
    swap.wait_recv()
    bh, bl = exact_gram(pt[last])
    gp[0] = jnp.where(lanes < 64, ah, pltpu.roll(bh, 64, 1))
    gp[1] = jnp.where(lanes < 64, al, pltpu.roll(bl, 64, 1))
    share = RANK // nx

    def rows_of(d):
        return pl.ds(pl.multiple_of(d * share, share), share)

    to_x = [send(gp.at[:, rows_of(x_peer(i))], gx.at[x], (gx_send, gx_recv), i, (x_peer(i) * nz + z, col))
            for i in range(1, nx)]
    gx[x] = gp[:, rows_of(x), :]

    for i in range(1, ny):
        gather[i - 1].wait_recv()
        m = 2 * y_peer(ny - i) + k
        forward.append(send(pt.at[m], pt.at[m], (fw_send, fw_recv), i, mate_id))

    def sum_pairs(ref, n):
        h, l = ref[0, 0], ref[0, 1]
        for i in range(1, n):
            h, l = add_pair(h, l, ref[i, 0], ref[i, 1])
        return h, l

    for c in to_x:
        c.wait_recv()
    h, l = sum_pairs(gx, nx)
    gz[z, 0] = h
    gz[z, 1] = l
    to_z = [send(gz.at[z], gz.at[z], (gz_send, gz_recv), i, (x * nz + z_peer(i), col)) for i in far_first]

    for c in forward:
        c.wait_recv()
    rows_t = tp.shape[1]
    for m in range(mats):
        t = cut_product(nn, pt[m], s_v[m])
        tp[0, m * RANK : (m + 1) * RANK, :] = t[:, 0:128]
        tp[1, m * RANK : (m + 1) * RANK, :] = t[:, 128:256]
    if rows_t > mats * RANK:
        tp[:, mats * RANK :, :] = jnp.zeros((2, rows_t - mats * RANK, 128), F32)

    piece = 2 * rows_t // nr
    per_half = nr // 2

    def piece_of(ref, d):
        return ref.at[d // per_half, pl.ds(pl.multiple_of((d % per_half) * piece, piece), piece)]

    hops = far_first + [0]
    t_x = {}
    for j in hops:
        zd = z_peer(j)
        for i in range(1, nx):
            xd = x_peer(i)
            t_x[i, j] = send(piece_of(tp, xd * nz + zd), xrecv.at[i, j], (tx_send, tx_recv), (i, j), (xd * nz + z, col))
    for m in range(mats):
        pw[m] = jnp.transpose(pt[m])

    for c in to_z:
        c.wait_recv()
    h, l = sum_pairs(gz, nz)
    ga[x, 0] = h
    ga[x, 1] = l
    to_a = [send(ga.at[x], ga.at[x], (ga_send, ga_recv), i, (x_peer(i) * nz + z, col)) for i in range(1, nx)]

    t_z = []
    for j in hops:
        zd = z_peer(j)
        acc = piece_of(tp, x * nz + zd)[...]
        for i in range(1, nx):
            t_x[i, j].wait_recv()
            acc = acc + xrecv[i, j]
        if j == 0:
            zrecv[0] = acc
        else:
            zsend[j] = acc
            t_z.append(send(zsend.at[j], zrecv.at[j], (tz_send, tz_recv), j, (x * nz + zd, col)))

    for c in to_a:
        c.wait_recv()
    for i in range(nx):
        mh[i * share : (i + 1) * share, :] = ga[i, 0]
        ml[i * share : (i + 1) * share, :] = ga[i, 1]
    factor_pair(mh, ml, 0, 32)

    for c in t_z:
        c.wait_recv()
    acc = zrecv[0]
    for j in range(1, nz):
        acc = acc + zrecv[j]
    mine = piece_of(tfull, row)
    mine[...] = acc
    a_z = {j: send(mine, mine, (az_send, az_recv), j, (x * nz + z_peer(j), col)) for j in far_first}
    a_x = []

    def pass_on(j):
        p = piece_of(tfull, x * nz + z_peer(nz - j))
        for i in range(1, nx):
            a_x.append(send(p, p, (ax_send, ax_recv), (i, j), (x_peer(i) * nz + z, col)))

    pass_on(0)
    factor_pair(mh, ml, 32, RANK)

    linv[own] = inverse_of(mh)
    spread = [send(linv.at[own], linv.at[own], (l_send, l_recv), i, (row, lax.rem(col + i, nc))) for i in range(1, nc)]
    for j in reversed(far_first):
        a_z[j].wait_recv()
        pass_on(j)
    linv[last] = pltpu.roll(linv[own], 64, 1)
    for c in spread:
        c.wait_recv()
    left = lax.broadcasted_iota(jnp.int32, (pw.shape[1], 3 * RANK), 1) < 2 * RANK
    for m in range(mats):
        li = linv[m][:, 0:RANK]
        q = nt(pw[m], jnp.concatenate([li, li, li], axis=0), HIGHEST)
        q1 = q.astype(BF16)
        q_out[m] = jnp.where(left, q1.astype(F32), q - q1.astype(F32)).astype(BF16)
    for c in a_x:
        c.wait_recv()

    squares = jnp.zeros((8, 128), F32)
    places = lax.broadcasted_iota(jnp.int32, (8, 256), 0)
    for pair in range(0, mats, 2):
        sqs = []
        for m in (pair, pair + 1):
            if m >= mats:
                sqs.append(jnp.zeros((RANK, 256), F32))
                continue
            at = slice(m * RANK, (m + 1) * RANK)
            t = jnp.concatenate([tfull[0, at, :], tfull[1, at, :]], axis=1)
            p = nn(linv[m][:, 0:RANK], t, HIGHEST)
            prod_out[m] = p
            sqs.append(p * p)
        ones = jnp.where(places == pair // 2, 1.0, 0.0)
        squares = squares + nt(ones, jnp.concatenate(sqs, axis=0), HIGHEST)
    sq[col] = squares
    to_all = [send(sq.at[col], sq.at[col], (sq_send, sq_recv), i, (row, lax.rem(col + i, nc))) for i in range(1, nc)]
    for m in range(mats):
        m_out[m] = s_v[m] - nn(q_out[m], stacked_pieces(prod_out[m] * (1.0 - DECAY)))
    for c in to_all:
        c.wait_recv()
    squares = sq[0]
    for i in range(1, nc):
        squares = squares + sq[i]
    scale_out[...] = jnp.transpose(1.0 / jnp.sqrt(squares * (1.0 / ff) + EPSILON))
    load_weight.wait()
    finish()


def stacked_pieces(p):
    p1 = p.astype(BF16)
    p2 = (p - p1.astype(F32)).astype(BF16)
    return jnp.concatenate([p1, p2, p1], axis=0)


def update_kernel(gain, w, mom, q, prod, scale, new_weight, new_mom, new_right, w_v, r_v, w_sem, m_sem, r_sem):
    mats = w.shape[0]
    move = pltpu.make_async_copy(mom, new_mom, m_sem)
    move.start()
    table = scale[...]
    moves = [move]
    for m in range(mats):
        column = table[(m % 2) * RANK : (m % 2 + 1) * RANK, m // 2 : m // 2 + 1]
        normed = prod[m] * column
        r_v[m] = normed
        c = pltpu.make_async_copy(r_v.at[m], new_right.at[m], r_sem.at[m])
        c.start()
        moves.append(c)
        w_v[m] = w[m] - nn(q[m], stacked_pieces(normed * gain))
        c = pltpu.make_async_copy(w_v.at[m], new_weight.at[m], w_sem.at[m])
        c.start()
        moves.append(c)
    for c in moves:
        c.wait()


def body(nx, nz, ny, depth, weight, grad, momentum, right):
    nr, nc = nx * nz, ny * 2
    mats, rows, cols = weight.shape
    ff = cols * nc
    rt = jnp.transpose(right, (1, 2, 0))
    piece = -(-2 * mats * RANK // nr)
    piece = -(-piece // 8) * 8
    rows_t = piece * nr // 2
    share = RANK // nx
    vmem = pl.BlockSpec(memory_space=pltpu.VMEM)
    hbm = pl.BlockSpec(memory_space=pltpu.HBM)
    dma = pltpu.SemaphoreType.DMA
    half = RANK // 2
    w, mom, q, prod, scale = pl.pallas_call(
        functools.partial(exchange_kernel, nx, nz, ny),
        out_shape=(
            jax.ShapeDtypeStruct((mats, rows, cols), F32),
            jax.ShapeDtypeStruct((mats, rows, cols), F32),
            jax.ShapeDtypeStruct((mats, rows, 3 * RANK), BF16),
            jax.ShapeDtypeStruct((mats, RANK, cols), F32),
            jax.ShapeDtypeStruct((128, 8), F32),
        ),
        in_specs=[hbm] * 4,
        out_specs=(vmem,) * 5,
        scratch_shapes=[
            pltpu.VMEM((mats, rows, cols), F32),
            pltpu.VMEM((mats, rows, cols), BF16),
            pltpu.VMEM((mats, RANK, cols), F32),
            pltpu.VMEM((mats, RANK, rows), F32),
            pltpu.VMEM((ny + 1, RANK, rows), F32),
            pltpu.VMEM((ny, RANK + half, rows), F32),
            pltpu.VMEM((ny, RANK + half, rows), F32),
            pltpu.VMEM((mats, RANK, rows), F32),
            pltpu.VMEM((mats, rows, RANK), F32),
            pltpu.VMEM((2, RANK, 128), F32),
            pltpu.VMEM((nx, 2, share, 128), F32),
            pltpu.VMEM((nz, 2, share, 128), F32),
            pltpu.VMEM((nx, 2, share, 128), F32),
            pltpu.VMEM((RANK, 128), F32),
            pltpu.VMEM((RANK, 128), F32),
            pltpu.VMEM((mats, RANK, 128), F32),
            pltpu.VMEM((2, rows_t, 128), F32),
            pltpu.VMEM((nx, nz, piece, 128), F32),
            pltpu.VMEM((nz, piece, 128), F32),
            pltpu.VMEM((nz, piece, 128), F32),
            pltpu.VMEM((2, rows_t, 128), F32),
            pltpu.VMEM((nc, 8, 128), F32),
            dma((2 * mats + 1,)),
            dma,
            dma((ny + 1,)), dma((ny + 1,)),
            dma((ny,)), dma((ny,)),
            dma((ny,)), dma((ny,)),
            dma((ny,)), dma((ny,)),
            dma((1,)), dma((1,)),
            dma((nx,)), dma((nx,)),
            dma((nz,)), dma((nz,)),
            dma((nx,)), dma((nx,)),
            dma((nx, nz)), dma((nx, nz)),
            dma((nz,)), dma((nz,)),
            dma((nz,)), dma((nz,)),
            dma((nx, nz)), dma((nx, nz)),
            dma((nc,)), dma((nc,)),
            dma((nc,)), dma((nc,)),
        ],
        compiler_params=pltpu.CompilerParams(
            collective_id=0, has_side_effects=True, vmem_limit_bytes=40 * 1024 * 1024
        ),
        name="exchange",
    )(*[pltpu.with_memory_space_constraint(v, pltpu.HBM) for v in (weight, grad, momentum, rt)])

    gain = math.sqrt(depth / ff)
    new_weight, new_momentum, new_right = pl.pallas_call(
        functools.partial(update_kernel, gain),
        out_shape=(
            jax.ShapeDtypeStruct(weight.shape, F32),
            jax.ShapeDtypeStruct(weight.shape, F32),
            jax.ShapeDtypeStruct((mats, RANK, cols), F32),
        ),
        in_specs=[vmem] * 5,
        out_specs=(hbm,) * 3,
        scratch_shapes=[
            pltpu.VMEM((mats, rows, cols), F32),
            pltpu.VMEM((mats, RANK, cols), F32),
            dma((mats,)),
            dma,
            dma((mats,)),
        ],
        compiler_params=pltpu.CompilerParams(vmem_limit_bytes=12 * 1024 * 1024),
        name="update",
    )(w, mom, q, prod, scale)
    return new_weight, new_momentum, jnp.transpose(new_right, (2, 0, 1))


def solution(mesh):
    nr, nc = mesh.shape["row"], mesh.shape["col"]
    nz = min(nr, 8)
    nx = nr // nz

    def run(weight, grad, momentum, right):
        return body(nx, nz, nc // 2, weight.shape[1] * nr, weight, grad, momentum, right)

    placed = P(None, "row", "col")
    return jax.shard_map(
        run,
        mesh=mesh,
        in_specs=(placed, placed, placed, P("col", None, None)),
        out_specs=(placed, placed, P("col", None, None)),
        check_vma=False,
    )
```

time: 108 us -> 66.8 us (0.62)
  Pallas kernels: 100 us -> 66.1 us
  local copies, waits for them, and re-layouts: 6.08 us -> 0 us
    pallas_call x1, Pallas kernels: 89.7 us -> 63.8 us  [body(): pl.pallas_call(functools.partial(exchange_kernel, nx, nz, ny), out_shape=...]
    pallas_call x1, Pallas kernels: 10.4 us -> 2.33 us  [body(): pl.pallas_call(functools.partial(update_kernel, gain), out_shape=(jax.Sha...]
    unnamed x12 -> x0, local copies, waits for them, and re-layouts: 6.08 us -> none
where the time goes in v2:
time: 66.8 us
  Pallas kernels  66.1 us (99%)
    pallas_call x1, Pallas kernels, body(): pl.pallas_call(functools.partial(exchange_kernel, nx, nz, ny), out_shape=...  63.8 us
    pallas_call x1, Pallas kernels, body(): pl.pallas_call(functools.partial(update_kernel, gain), out_shape=(jax.Sha...  2.33 us

profile of v2, /device:TPU:1, one launch (start us, length us, event | category | flops | bytes accessed | tf_op | source)
XLA Modules:
  0.0 66.8 jit_solution(16883297260073054761)
XLA Ops:
  0.6 63.8 %exchange.1 = (f32[9,224,256]{2,1,0:T(8,128)S(1)}, f32[9,224,256]{2,1,0:T(8,128)S(1)}, bf16[9,224,192]{2,1,0:T(8,128)(2,1)S(1)}, f32[9,64,256]{2,1,0:T(8,128)S(1)}, f32[128,8]{1,0:T(8,128)S(1)}) custom-call(f32[9,224,256]{2,1,0:T(8,128)} %weight.1, bf16[9,224,256]{2,1,0:T(8,128)(2,1)} %grad.1, f32[9,224,256]{2,1,0:T(8,128)} %mom.1, f32[9,64,256]{2,1,0:T(8,128)} %bitcast.2), custom_call_target="tpu_custom_call" | custom-call | tf_op jit(solution)/shard_map/exchange/pallas_call | solution.py:468
  64.4 2.3 %update.1 = (f32[9,224,256]{2,1,0:T(8,128)}, f32[9,224,256]{2,1,0:T(8,128)}, f32[9,64,256]{2,1,0:T(8,128)}) custom-call(f32[9,224,256]{2,1,0:T(8,128)S(1)} %get-tuple-element.11.w, f32[9,224,256]{2,1,0:T(8,128)S(1)} %get-tuple-element.12.mom, bf16[9,224,192]{2,1,0:T(8,128)(2,1)S(1)} %get-tuple-element.13.q, f32[9,64,256]{2,1,0:T(8,128)S(1)} %get-tuple-element.14.prod, ...), custom_call_target="tpu_custom_call" | custom-call | tf_op jit(solution)/shard_map/update/pallas_call | solution.py:526

commit v3 on v2

--- a/solution.py
+++ b/solution.py
@@ -238,10 +238,10 @@
     for n, i in enumerate(turns):
         m = 2 * y_peer(i) + (1 - k)
         power(m)
-        if n == 0:
-            pl.semaphore_wait(barrier, len(peers))
-        to_mate[i] = send(part.at[m], mate.at[i], mate_sems, i, mate_id)
     power(last)
+    pl.semaphore_wait(barrier, len(peers))
+    for i in turns:
+        to_mate[i] = send(part.at[2 * y_peer(i) + (1 - k)], mate.at[i], mate_sems, i, mate_id)
     other_rows = pl.ds(pl.multiple_of((1 - k) * half, half), half)
     my_rows = pl.ds(pl.multiple_of(k * half, half), half)
     to_mate[ny] = send(part.at[last, other_rows], mate.at[ny, pl.ds(0, half)], mate_sems, ny, mate_id)
@@ -273,7 +273,7 @@
     swap = send(pt.at[last, my_rows], pt.at[last, my_rows], (h_send, h_recv), 0, mate_id)
     pt[own] = total[0:RANK]
     gather = [send(pt.at[own], pt.at[own], (ag_send, ag_recv), i, (row, 2 * y_peer(i) + k)) for i in range(1, ny)]
-    forward = [send(pt.at[own], pt.at[own], (fw_send, fw_recv), 0, mate_id)]
+    forward = {0: send(pt.at[own], pt.at[own], (fw_send, fw_recv), 0, mate_id)}
 
     lanes = lax.broadcasted_iota(jnp.int32, (RANK, 128), 1)
     ah, al = exact_gram(total[0:RANK])
@@ -290,10 +290,43 @@
             for i in range(1, nx)]
     gx[x] = gp[:, rows_of(x), :]
 
-    for i in range(1, ny):
-        gather[i - 1].wait_recv()
-        m = 2 * y_peer(ny - i) + k
-        forward.append(send(pt.at[m], pt.at[m], (fw_send, fw_recv), i, mate_id))
+    pairs = tp.shape[0]
+    depth = tp.shape[2]
+    t_x = {}
+
+    def times(m, q, e):
+        t = cut_product(nn, pt[m], s_v[m])
+        at, to = e * RANK // depth, e * RANK % depth
+        for h in range(2):
+            tp[q, h * nx // 2 + at, to : to + RANK, :] = t[:, h * 128 : (h + 1) * 128]
+
+    def block_out(turn, q):
+        for i in range(1, nx):
+            t_x[turn, i] = send(tp.at[q, x_peer(i)], xrecv.at[turn, i], (tx_send, tx_recv), (turn, i),
+                                (x_peer(i) * nz + z, col))
+
+    def times_pair(d):
+        q = y_peer(d)
+        times(2 * q, q, 0)
+        times(2 * q + 1, q, 1)
+        block_out(d, q)
+
+    arrivals = sorted(range(1, ny), key=lambda d: min(d, ny - d))
+
+    def pass_power(d):
+        gather[ny - d - 1].wait_recv()
+        m = 2 * y_peer(d) + k
+        forward[d] = send(pt.at[m], pt.at[m], (fw_send, fw_recv), d, mate_id)
+
+    at, to = RANK // depth, RANK % depth
+    for h in range(2):
+        tp[pairs - 1, h * nx // 2 + at, to : to + RANK, :] = jnp.zeros((RANK, 128), F32)
+    times(last, pairs - 1, 0)
+    block_out(ny, pairs - 1)
+    forward[0].wait_recv()
+    times_pair(0)
+    for d in arrivals[:-1]:
+        pass_power(d)
 
     def sum_pairs(ref, n):
         h, l = ref[0, 0], ref[0, 1]
@@ -307,32 +340,23 @@
     gz[z, 0] = h
     gz[z, 1] = l
     to_z = [send(gz.at[z], gz.at[z], (gz_send, gz_recv), i, (x * nz + z_peer(i), col)) for i in far_first]
-
-    for c in forward:
-        c.wait_recv()
-    rows_t = tp.shape[1]
-    for m in range(mats):
-        t = cut_product(nn, pt[m], s_v[m])
-        tp[0, m * RANK : (m + 1) * RANK, :] = t[:, 0:128]
-        tp[1, m * RANK : (m + 1) * RANK, :] = t[:, 128:256]
-    if rows_t > mats * RANK:
-        tp[:, mats * RANK :, :] = jnp.zeros((2, rows_t - mats * RANK, 128), F32)
-
-    piece = 2 * rows_t // nr
-    per_half = nr // 2
-
-    def piece_of(ref, d):
-        return ref.at[d // per_half, pl.ds(pl.multiple_of((d % per_half) * piece, piece), piece)]
-
-    hops = far_first + [0]
-    t_x = {}
-    for j in hops:
-        zd = z_peer(j)
-        for i in range(1, nx):
-            xd = x_peer(i)
-            t_x[i, j] = send(piece_of(tp, xd * nz + zd), xrecv.at[i, j], (tx_send, tx_recv), (i, j), (xd * nz + z, col))
+    for n, d in enumerate(arrivals):
+        if n == ny - 2:
+            pass_power(d)
+        forward[d].wait_recv()
+        times_pair(d)
     for m in range(mats):
         pw[m] = jnp.transpose(pt[m])
+
+    for d in [ny, 0] + arrivals:
+        q = pairs - 1 if d == ny else y_peer(d)
+        acc = tp[q, x]
+        for i in range(1, nx):
+            t_x[d, i].wait_recv()
+            acc = acc + xrecv[d, i]
+        zsend[q] = acc.reshape(zsend.shape[1:])
+    t_z = [send(zsend.at[:, z_peer(j)], zrecv.at[j], (tz_send, tz_recv), j, (x * nz + z_peer(j), col)) for j in far_first]
+    zrecv[0] = zsend[:, z]
 
     for c in to_z:
         c.wait_recv()
@@ -341,49 +365,41 @@
     ga[x, 1] = l
     to_a = [send(ga.at[x], ga.at[x], (ga_send, ga_recv), i, (x_peer(i) * nz + z, col)) for i in range(1, nx)]
 
-    t_z = []
-    for j in hops:
-        zd = z_peer(j)
-        acc = piece_of(tp, x * nz + zd)[...]
+    for c in t_z:
+        c.wait_recv()
+    acc = zrecv[0]
+    for j in range(1, nz):
+        acc = acc + zrecv[j]
+    tfull[:, x, z] = acc
+    a_z = {j: send(tfull.at[:, x, z], tfull.at[:, x, z], (az_send, az_recv), j, (x * nz + z_peer(j), col))
+           for j in far_first}
+    a_x = []
+
+    def pass_on(j):
+        p = tfull.at[:, x, z_peer(nz - j)] if j else tfull.at[:, x, z]
         for i in range(1, nx):
-            t_x[i, j].wait_recv()
-            acc = acc + xrecv[i, j]
-        if j == 0:
-            zrecv[0] = acc
-        else:
-            zsend[j] = acc
-            t_z.append(send(zsend.at[j], zrecv.at[j], (tz_send, tz_recv), j, (x * nz + zd, col)))
-
+            a_x.append(send(p, p, (ax_send, ax_recv), (i, j), (x_peer(i) * nz + z, col)))
+
+    pass_on(0)
     for c in to_a:
         c.wait_recv()
     for i in range(nx):
         mh[i * share : (i + 1) * share, :] = ga[i, 0]
         ml[i * share : (i + 1) * share, :] = ga[i, 1]
+    near_first = far_first[::-1]
+    early = (nz - 1) // 2
     factor_pair(mh, ml, 0, 32)
-
-    for c in t_z:
-        c.wait_recv()
-    acc = zrecv[0]
-    for j in range(1, nz):
-        acc = acc + zrecv[j]
-    mine = piece_of(tfull, row)
-    mine[...] = acc
-    a_z = {j: send(mine, mine, (az_send, az_recv), j, (x * nz + z_peer(j), col)) for j in far_first}
-    a_x = []
-
-    def pass_on(j):
-        p = piece_of(tfull, x * nz + z_peer(nz - j))
-        for i in range(1, nx):
-            a_x.append(send(p, p, (ax_send, ax_recv), (i, j), (x_peer(i) * nz + z, col)))
-
-    pass_on(0)
-    factor_pair(mh, ml, 32, RANK)
+    for j in near_first[:early]:
+        a_z[j].wait_recv()
+        pass_on(j)
+    factor_pair(mh, ml, 32, 48)
+    for j in near_first[early:]:
+        a_z[j].wait_recv()
+        pass_on(j)
+    factor_pair(mh, ml, 48, RANK)
 
     linv[own] = inverse_of(mh)
     spread = [send(linv.at[own], linv.at[own], (l_send, l_recv), i, (row, lax.rem(col + i, nc))) for i in range(1, nc)]
-    for j in reversed(far_first):
-        a_z[j].wait_recv()
-        pass_on(j)
     linv[last] = pltpu.roll(linv[own], 64, 1)
     for c in spread:
         c.wait_recv()
@@ -404,8 +420,8 @@
             if m >= mats:
                 sqs.append(jnp.zeros((RANK, 256), F32))
                 continue
-            at = slice(m * RANK, (m + 1) * RANK)
-            t = jnp.concatenate([tfull[0, at, :], tfull[1, at, :]], axis=1)
+            at, to = (m % 2) * RANK // depth, (m % 2) * RANK % depth
+            t = jnp.concatenate([tfull[m // 2, h * nx // 2 + at].reshape(depth, 128)[to : to + RANK] for h in range(2)], axis=1)
             p = nn(linv[m][:, 0:RANK], t, HIGHEST)
             prod_out[m] = p
             sqs.append(p * p)
@@ -457,9 +473,9 @@
     mats, rows, cols = weight.shape
     ff = cols * nc
     rt = jnp.transpose(right, (1, 2, 0))
-    piece = -(-2 * mats * RANK // nr)
-    piece = -(-piece // 8) * 8
-    rows_t = piece * nr // 2
+    pairs = (mats + 1) // 2
+    block = 256 // nx
+    tile = block // nz
     share = RANK // nx
     vmem = pl.BlockSpec(memory_space=pltpu.VMEM)
     hbm = pl.BlockSpec(memory_space=pltpu.HBM)
@@ -493,11 +509,11 @@
             pltpu.VMEM((RANK, 128), F32),
             pltpu.VMEM((RANK, 128), F32),
             pltpu.VMEM((mats, RANK, 128), F32),
-            pltpu.VMEM((2, rows_t, 128), F32),
-            pltpu.VMEM((nx, nz, piece, 128), F32),
-            pltpu.VMEM((nz, piece, 128), F32),
-            pltpu.VMEM((nz, piece, 128), F32),
-            pltpu.VMEM((2, rows_t, 128), F32),
+            pltpu.VMEM((pairs, nx, block, 128), F32),
+            pltpu.VMEM((pairs, nx, block, 128), F32),
+            pltpu.VMEM((pairs, nz, tile, 128), F32),
+            pltpu.VMEM((nz, pairs, tile, 128), F32),
+            pltpu.VMEM((pairs, nx, nz, tile, 128), F32),
             pltpu.VMEM((nc, 8, 128), F32),
             dma((2 * mats + 1,)),
             dma,
@@ -509,7 +525,7 @@
             dma((nx,)), dma((nx,)),
             dma((nz,)), dma((nz,)),
             dma((nx,)), dma((nx,)),
-            dma((nx, nz)), dma((nx, nz)),
+            dma((pairs, nx)), dma((pairs, nx)),
             dma((nz,)), dma((nz,)),
             dma((nz,)), dma((nz,)),
             dma((nx, nz)), dma((nx, nz)),

time: 66.8 us -> 64.9 us (0.972)
  Pallas kernels: 66.1 us -> 64.1 us
    pallas_call x1, Pallas kernels: 63.8 us -> 61.8 us  [body(): pl.pallas_call(functools.partial(exchange_kernel, nx, nz, ny), out_shape=...]
where the time goes in v3:
time: 64.9 us; the launch traced here: 64.8 us
  Pallas kernels  64.1 us (99%)
    pallas_call x1, Pallas kernels, body(): pl.pallas_call(functools.partial(exchange_kernel, nx, nz, ny), out_shape=...  61.8 us
    pallas_call x1, Pallas kernels, body(): pl.pallas_call(functools.partial(update_kernel, gain), out_shape=(jax.Sha...  2.33 us

profile of v3, /device:TPU:1, one launch (start us, length us, event | category | flops | bytes accessed | tf_op | source)
XLA Modules:
  0.0 64.8 jit_solution(15474617331916353940)
XLA Ops:
  0.6 61.8 %exchange.1 = (f32[9,224,256]{2,1,0:T(8,128)S(1)}, f32[9,224,256]{2,1,0:T(8,128)S(1)}, bf16[9,224,192]{2,1,0:T(8,128)(2,1)S(1)}, f32[9,64,256]{2,1,0:T(8,128)S(1)}, f32[128,8]{1,0:T(8,128)S(1)}) custom-call(f32[9,224,256]{2,1,0:T(8,128)} %weight.1, bf16[9,224,256]{2,1,0:T(8,128)(2,1)} %grad.1, f32[9,224,256]{2,1,0:T(8,128)} %mom.1, f32[9,64,256]{2,1,0:T(8,128)} %bitcast.2), custom_call_target="tpu_custom_call" | custom-call | tf_op jit(solution)/shard_map/exchange/pallas_call | solution.py:484
  62.4 2.3 %update.1 = (f32[9,224,256]{2,1,0:T(8,128)}, f32[9,224,256]{2,1,0:T(8,128)}, f32[9,64,256]{2,1,0:T(8,128)}) custom-call(f32[9,224,256]{2,1,0:T(8,128)S(1)} %get-tuple-element.11.w, f32[9,224,256]{2,1,0:T(8,128)S(1)} %get-tuple-element.12.mom, bf16[9,224,192]{2,1,0:T(8,128)(2,1)S(1)} %get-tuple-element.13.q, f32[9,64,256]{2,1,0:T(8,128)S(1)} %get-tuple-element.14.prod, ...), custom_call_target="tpu_custom_call" | custom-call | tf_op jit(solution)/shard_map/update/pallas_call | solution.py:542

commit v4 on v3

--- a/solution.py
+++ b/solution.py
@@ -107,64 +107,102 @@
     return gh * unit * across, gl * unit * across
 
 
-def factor_block(mh, ml, first, count, begin, end):
+def mul_pair(ah, al, bh, bl):
+    p, e = two_prod(ah, bh)
+    return p, e + (ah * bl + al * bh)
+
+
+def factor_block(mh, ml, first):
+    count = RANK - first
     rows = lax.broadcasted_iota(jnp.int32, (count, 128), 0) + first
     lanes = lax.broadcasted_iota(jnp.int32, (count, 128), 1)
     half = jnp.where(lanes >= 64, 64, 0)
     column = lanes - half
-
-    def step(k, carry):
-        ah, al = mh[first:, :], ml[first:, :]
-        rh, rl = mh[pl.ds(k, 1), :], ml[pl.ds(k, 1), :]
-        index = half + k
-        ch = jnp.take_along_axis(ah, index, axis=1)
-        cl = jnp.take_along_axis(al, index, axis=1)
-        dh = jnp.take_along_axis(jnp.broadcast_to(rh, (8, 128)), index[0:8], axis=1)[0:1]
-        dl = jnp.take_along_axis(jnp.broadcast_to(rl, (8, 128)), index[0:8], axis=1)[0:1]
+    h, l = mh[first:, :], ml[first:, :]
+
+    def lane(v, k):
+        return jnp.take_along_axis(jnp.broadcast_to(v, (8, 128)), half[0:8] + k, axis=1)[0:1]
+
+    for k in range(first, first + 8, 2):
+        i = k - first
+        r1h, r1l = h[i : i + 1], l[i : i + 1]
+        r2h, r2l = h[i + 1 : i + 2], l[i + 1 : i + 2]
+        ah, al = lane(r1h, k), lane(r1l, k)
+        bh, bl = lane(r1h, k + 1), lane(r1l, k + 1)
+        ch, cl = lane(r2h, k + 1), lane(r2l, k + 1)
+        p1, e1 = mul_pair(ah, al, ch, cl)
+        p2, e2 = mul_pair(bh, bl, bh, bl)
+        dh, dl = add_pair(p1, e1, -p2, -e2)
         inv = 1.0 / dh
         p, e = two_prod(dh, inv)
         inv_low = inv * (((1.0 - p) - e) - dl * inv)
-        p, e = two_prod(ch, inv)
-        t = e + (ch * inv_low + cl * inv)
-        nh = p + t
-        nl = t - (nh - p)
-        later = rows > k
-        nh = jnp.where(later, nh, 0.0)
-        nl = jnp.where(later, nl, 0.0)
-        here = column == k
-        rh = jnp.where(here[0:1], 1.0, rh)
-        rl = jnp.where(here[0:1], 0.0, rl)
+        p1, e1 = mul_pair(r1h, r1l, ch, cl)
+        p2, e2 = mul_pair(r2h, r2l, bh, bl)
+        t1h, t1l = add_pair(p1, e1, -p2, -e2)
+        p1, e1 = mul_pair(r2h, r2l, ah, al)
+        p2, e2 = mul_pair(r1h, r1l, bh, bl)
+        t2h, t2l = add_pair(p1, e1, -p2, -e2)
+        n1h, n1l = mul_pair(t1h, t1l, inv, inv_low)
+        n2h, n2l = mul_pair(t2h, t2l, inv, inv_low)
+        later = rows > k + 1
+
+        def spread(v):
+            out = jnp.take_along_axis(jnp.broadcast_to(v, (count, 128)), half + rows, axis=1)
+            return jnp.where(later, out, 0.0)
+
+        n1h, n1l, n2h, n2l = spread(n1h), spread(n1l), spread(n2h), spread(n2l)
+        here1, here2 = column == k, column == k + 1
+        here = here1 | here2
+        r1h = jnp.where(here1[0:1], 1.0, jnp.where(here2[0:1], 0.0, r1h))
+        r2h = jnp.where(here2[0:1], 1.0, jnp.where(here1[0:1], 0.0, r2h))
+        r1l = jnp.where(here[0:1], 0.0, r1l)
+        r2l = jnp.where(here[0:1], 0.0, r2l)
         clear = here & later
-        ah = jnp.where(clear, 0.0, ah)
-        al = jnp.where(clear, 0.0, al)
-        p, e = two_prod(nh, rh)
-        q = e + (nh * rl + nl * rh)
-        s, t = two_sum(ah, -p)
-        t = t + (al - q)
+        h = jnp.where(clear, 0.0, h)
+        l = jnp.where(clear, 0.0, l)
+        p, q = mul_pair(n1h, n1l, r1h, r1l)
+        s, t = two_sum(h, -p)
+        p2, q2 = mul_pair(n2h, n2l, r2h, r2l)
+        s, t2 = two_sum(s, -p2)
+        t = (t + t2) + (l - (q + q2))
         h = s + t
-        mh[first:, :] = h
-        ml[first:, :] = t - (h - s)
-        return carry
-
-    lax.fori_loop(begin, end, step, 0)
+        l = t - (h - s)
+    mh[first:, :] = h
+    ml[first:, :] = l
 
 
 def factor_pair(mh, ml, begin, end):
     for first in range(begin, end, 8):
-        factor_block(mh, ml, first, RANK - first, first, first + 8)
-
-
-def inverse_of(mh):
+        factor_block(mh, ml, first)
+
+
+def inverse_of(mh, ml):
     m = mh[...]
     rows = lax.broadcasted_iota(jnp.int32, (RANK, 128), 0)
     lanes = lax.broadcasted_iota(jnp.int32, (RANK, 128), 1)
     left = lanes < 64
     column = jnp.where(left, lanes, lanes - 64)
-    diagonal = jnp.where(column == rows, m, 0.0)
-    da = jnp.sum(jnp.where(left, diagonal, 0.0), axis=1, keepdims=True)
-    db = jnp.sum(jnp.where(left, 0.0, diagonal), axis=1, keepdims=True)
-    root = 1.0 / jnp.sqrt(jnp.where(left, da, db))
-    return jnp.where(column < rows, m * root, jnp.where(column == rows, root, 0.0))
+    odd = (rows & 1) == 1
+
+    def pick(v, mask):
+        v = jnp.where(mask, v, 0.0)
+        a = jnp.sum(jnp.where(left, v, 0.0), axis=1, keepdims=True)
+        b = jnp.sum(jnp.where(left, 0.0, v), axis=1, keepdims=True)
+        return jnp.where(left, a, b)
+
+    same, next_to = column == rows, column == (rows ^ 1)
+    ch, cl = pick(m, same), pick(ml[...], same)
+    bh, bl = pick(m, next_to), pick(ml[...], next_to)
+    ah, al = pltpu.roll(ch, 1, 0), pltpu.roll(cl, 1, 0)
+    inv = 1.0 / ah
+    p, e = two_prod(ah, inv)
+    rh, rl = mul_pair(bh, bl, inv, inv * (((1.0 - p) - e) - al * inv))
+    p, e = mul_pair(rh, rl, bh, bl)
+    ph, _ = add_pair(ch, cl, -p, -e)
+    root = 1.0 / jnp.sqrt(jnp.where(odd, ph, ch))
+    ratio = jnp.where(odd, rh, 0.0)
+    unit = jnp.where(column < rows - (rows & 1), m, jnp.where(column == rows, 1.0, 0.0))
+    return (unit - ratio * pltpu.roll(unit, 1, 0)) * root
 
 
 def exchange_kernel(nx, nz, ny, weight, grad, mom, right, w_out, m_out, q_out, prod_out, scale_out, s_v, g_v, r_v, part,
@@ -387,31 +425,32 @@
         mh[i * share : (i + 1) * share, :] = ga[i, 0]
         ml[i * share : (i + 1) * share, :] = ga[i, 1]
     near_first = far_first[::-1]
-    early = (nz - 1) // 2
+
+    def pass_next(n):
+        for j in near_first[:n]:
+            a_z[j].wait_recv()
+            pass_on(j)
+        del near_first[:n]
+
     factor_pair(mh, ml, 0, 32)
-    for j in near_first[:early]:
-        a_z[j].wait_recv()
-        pass_on(j)
+    pass_next(2)
     factor_pair(mh, ml, 32, 48)
-    for j in near_first[early:]:
-        a_z[j].wait_recv()
-        pass_on(j)
+    pass_next(2)
     factor_pair(mh, ml, 48, RANK)
 
-    linv[own] = inverse_of(mh)
+    inverse = inverse_of(mh, ml)
+    low = pltpu.roll(inverse[half:], 64, 1)
+    first_lanes = lax.broadcasted_iota(jnp.int32, (half, 128), 1) < 64
+    linv[own] = jnp.where(first_lanes, inverse[0:half], low)
+    linv[last] = jnp.where(first_lanes, pltpu.roll(inverse[0:half], 64, 1), inverse[half:])
     spread = [send(linv.at[own], linv.at[own], (l_send, l_recv), i, (row, lax.rem(col + i, nc))) for i in range(1, nc)]
-    linv[last] = pltpu.roll(linv[own], 64, 1)
-    for c in spread:
+    pass_next(nz)
+
+    def inverse_at(m):
+        return jnp.concatenate([linv[m][:, 0:RANK], linv[m][:, RANK:]], axis=0)
+
+    for c in spread + a_x:
         c.wait_recv()
-    left = lax.broadcasted_iota(jnp.int32, (pw.shape[1], 3 * RANK), 1) < 2 * RANK
-    for m in range(mats):
-        li = linv[m][:, 0:RANK]
-        q = nt(pw[m], jnp.concatenate([li, li, li], axis=0), HIGHEST)
-        q1 = q.astype(BF16)
-        q_out[m] = jnp.where(left, q1.astype(F32), q - q1.astype(F32)).astype(BF16)
-    for c in a_x:
-        c.wait_recv()
-
     squares = jnp.zeros((8, 128), F32)
     places = lax.broadcasted_iota(jnp.int32, (8, 256), 0)
     for pair in range(0, mats, 2):
@@ -422,15 +461,21 @@
                 continue
             at, to = (m % 2) * RANK // depth, (m % 2) * RANK % depth
             t = jnp.concatenate([tfull[m // 2, h * nx // 2 + at].reshape(depth, 128)[to : to + RANK] for h in range(2)], axis=1)
-            p = nn(linv[m][:, 0:RANK], t, HIGHEST)
+            p = nn(inverse_at(m), t, HIGHEST)
             prod_out[m] = p
             sqs.append(p * p)
         ones = jnp.where(places == pair // 2, 1.0, 0.0)
         squares = squares + nt(ones, jnp.concatenate(sqs, axis=0), HIGHEST)
     sq[col] = squares
     to_all = [send(sq.at[col], sq.at[col], (sq_send, sq_recv), i, (row, lax.rem(col + i, nc))) for i in range(1, nc)]
+    left = lax.broadcasted_iota(jnp.int32, (pw.shape[1], 3 * RANK), 1) < 2 * RANK
     for m in range(mats):
-        m_out[m] = s_v[m] - nn(q_out[m], stacked_pieces(prod_out[m] * (1.0 - DECAY)))
+        li = inverse_at(m)
+        q = nt(pw[m], jnp.concatenate([li, li, li], axis=0), HIGHEST)
+        q1 = q.astype(BF16)
+        pieces = jnp.where(left, q1.astype(F32), q - q1.astype(F32)).astype(BF16)
+        q_out[m] = pieces
+        m_out[m] = s_v[m] - nn(pieces, stacked_pieces(prod_out[m] * (1.0 - DECAY)))
     for c in to_all:
         c.wait_recv()
     squares = sq[0]
@@ -508,7 +553,7 @@
             pltpu.VMEM((nx, 2, share, 128), F32),
             pltpu.VMEM((RANK, 128), F32),
             pltpu.VMEM((RANK, 128), F32),
-            pltpu.VMEM((mats, RANK, 128), F32),
+            pltpu.VMEM((mats, half, 128), F32),
             pltpu.VMEM((pairs, nx, block, 128), F32),
             pltpu.VMEM((pairs, nx, block, 128), F32),
             pltpu.VMEM((pairs, nz, tile, 128), F32),

time: 64.9 us -> 62.5 us (0.963)
  Pallas kernels: 64.1 us -> 61.8 us
    pallas_call x1, Pallas kernels: 61.8 us -> 59.5 us  [body(): pl.pallas_call(functools.partial(exchange_kernel, nx, nz, ny), out_shape=...]
where the time goes in v4:
time: 62.5 us
  Pallas kernels  61.8 us (99%)
  between operations  0.64 us (1%)
    pallas_call x1, Pallas kernels, body(): pl.pallas_call(functools.partial(exchange_kernel, nx, nz, ny), out_shape=...  59.5 us
    pallas_call x1, Pallas kernels, body(): pl.pallas_call(functools.partial(update_kernel, gain), out_shape=(jax.Sha...  2.33 us

profile of v4, /device:TPU:1, one launch (start us, length us, event | category | flops | bytes accessed | tf_op | source)
XLA Modules:
  0.0 62.5 jit_solution(17053586005290497931)
XLA Ops:
  0.6 59.5 %exchange.1 = (f32[9,224,256]{2,1,0:T(8,128)S(1)}, f32[9,224,256]{2,1,0:T(8,128)S(1)}, bf16[9,224,192]{2,1,0:T(8,128)(2,1)S(1)}, f32[9,64,256]{2,1,0:T(8,128)S(1)}, f32[128,8]{1,0:T(8,128)S(1)}) custom-call(f32[9,224,256]{2,1,0:T(8,128)} %weight.1, bf16[9,224,256]{2,1,0:T(8,128)(2,1)} %grad.1, f32[9,224,256]{2,1,0:T(8,128)} %mom.1, f32[9,64,256]{2,1,0:T(8,128)} %bitcast.2), custom_call_target="tpu_custom_call" | custom-call | tf_op jit(solution)/shard_map/exchange/pallas_call | solution.py:529
  60.1 2.3 %update.1 = (f32[9,224,256]{2,1,0:T(8,128)}, f32[9,224,256]{2,1,0:T(8,128)}, f32[9,64,256]{2,1,0:T(8,128)}) custom-call(f32[9,224,256]{2,1,0:T(8,128)S(1)} %get-tuple-element.11.w, f32[9,224,256]{2,1,0:T(8,128)S(1)} %get-tuple-element.12.mom, bf16[9,224,192]{2,1,0:T(8,128)(2,1)S(1)} %get-tuple-element.13.q, f32[9,64,256]{2,1,0:T(8,128)S(1)} %get-tuple-element.14.prod, ...), custom_call_target="tpu_custom_call" | custom-call | tf_op jit(solution)/shard_map/update/pallas_call | solution.py:587

commit v5 on v4

--- a/solution.py
+++ b/solution.py
@@ -9,7 +9,6 @@
 from jax.sharding import PartitionSpec as P
 
 MESH = pl.DeviceIdType.MESH
-HIGHEST = lax.Precision.HIGHEST
 F32 = jnp.float32
 BF16 = jnp.bfloat16
 
@@ -70,6 +69,16 @@
     q = dot(jnp.concatenate([a1, a2], axis=0), b2)
     r = dot(a1, b3)
     return p[0:RANK] + ((p[RANK : 2 * RANK] + q[0:RANK]) + (p[2 * RANK :] + q[RANK:] + r))
+
+
+def six_left(a):
+    a1, a2, a3 = cut(a)
+    return jnp.concatenate([a1, a2, a1, a3, a2, a1], axis=1)
+
+
+def six_right(a, axis):
+    a1, a2, a3 = cut(a)
+    return jnp.concatenate([a1, a1, a2, a1, a2, a3], axis=axis)
 
 
 def round_int(v):
@@ -112,63 +121,71 @@
     return p, e + (ah * bl + al * bh)
 
 
+def sub_pairs(h, l, m1, r1, m2, r2):
+    p, q = mul_pair(*m1, *r1)
+    s, e = two_sum(h, -p)
+    p2, q2 = mul_pair(*m2, *r2)
+    s, e2 = two_sum(s, -p2)
+    e = (e + e2) + (l - (q + q2))
+    h = s + e
+    return h, e - (h - s)
+
+
+def cross(a, b, c, d):
+    p1, e1 = mul_pair(*a, *b)
+    p2, e2 = mul_pair(*c, *d)
+    return add_pair(p1, e1, -p2, -e2)
+
+
 def factor_block(mh, ml, first):
-    count = RANK - first
-    rows = lax.broadcasted_iota(jnp.int32, (count, 128), 0) + first
-    lanes = lax.broadcasted_iota(jnp.int32, (count, 128), 1)
+    tiles = (RANK - first) // 8
+    rows = lax.broadcasted_iota(jnp.int32, (8, 128), 0)
+    lanes = lax.broadcasted_iota(jnp.int32, (8, 128), 1)
     half = jnp.where(lanes >= 64, 64, 0)
     column = lanes - half
-    h, l = mh[first:, :], ml[first:, :]
-
-    def lane(v, k):
-        return jnp.take_along_axis(jnp.broadcast_to(v, (8, 128)), half[0:8] + k, axis=1)[0:1]
-
-    for k in range(first, first + 8, 2):
-        i = k - first
-        r1h, r1l = h[i : i + 1], l[i : i + 1]
-        r2h, r2l = h[i + 1 : i + 2], l[i + 1 : i + 2]
-        ah, al = lane(r1h, k), lane(r1l, k)
-        bh, bl = lane(r1h, k + 1), lane(r1l, k + 1)
-        ch, cl = lane(r2h, k + 1), lane(r2l, k + 1)
-        p1, e1 = mul_pair(ah, al, ch, cl)
-        p2, e2 = mul_pair(bh, bl, bh, bl)
-        dh, dl = add_pair(p1, e1, -p2, -e2)
+    m = [(mh[first + 8 * t : first + 8 * t + 8, :], ml[first + 8 * t : first + 8 * t + 8, :]) for t in range(tiles)]
+
+    def row(v, i):
+        return tuple(jnp.broadcast_to(part[i : i + 1], (8, 128)) for part in v)
+
+    def masked(mask, v):
+        return tuple(jnp.where(mask, part, 0.0) for part in v)
+
+    own = [tuple(jnp.take_along_axis(part, half + (first + j), axis=1) for part in m[0]) for j in range(8)]
+    steps = []
+    for i in range(0, 8, 2):
+        k = first + i
+        c1, c2 = own[i], own[i + 1]
+        a, b, c = row(c1, i), row(c2, i), row(c2, i + 1)
+        dh, dl = cross(a, c, b, b)
         inv = 1.0 / dh
         p, e = two_prod(dh, inv)
-        inv_low = inv * (((1.0 - p) - e) - dl * inv)
-        p1, e1 = mul_pair(r1h, r1l, ch, cl)
-        p2, e2 = mul_pair(r2h, r2l, bh, bl)
-        t1h, t1l = add_pair(p1, e1, -p2, -e2)
-        p1, e1 = mul_pair(r2h, r2l, ah, al)
-        p2, e2 = mul_pair(r1h, r1l, bh, bl)
-        t2h, t2l = add_pair(p1, e1, -p2, -e2)
-        n1h, n1l = mul_pair(t1h, t1l, inv, inv_low)
-        n2h, n2l = mul_pair(t2h, t2l, inv, inv_low)
-        later = rows > k + 1
-
-        def spread(v):
-            out = jnp.take_along_axis(jnp.broadcast_to(v, (count, 128)), half + rows, axis=1)
-            return jnp.where(later, out, 0.0)
-
-        n1h, n1l, n2h, n2l = spread(n1h), spread(n1l), spread(n2h), spread(n2l)
+        inv = (inv, inv * (((1.0 - p) - e) - dl * inv))
+        later = rows > i + 1
+        n1 = masked(later, mul_pair(*cross(c1, c, c2, b), *inv))
+        n2 = masked(later, mul_pair(*cross(c2, a, c1, b), *inv))
+        for j in range(i + 2, 8):
+            own[j] = sub_pairs(*own[j], n1, row(own[j], i), n2, row(own[j], i + 1))
+        r1, r2 = row(m[0], i), row(m[0], i + 1)
+        w1 = mul_pair(*cross(r1, c, r2, b), *inv)
+        w2 = mul_pair(*cross(r2, a, r1, b), *inv)
         here1, here2 = column == k, column == k + 1
         here = here1 | here2
-        r1h = jnp.where(here1[0:1], 1.0, jnp.where(here2[0:1], 0.0, r1h))
-        r2h = jnp.where(here2[0:1], 1.0, jnp.where(here1[0:1], 0.0, r2h))
-        r1l = jnp.where(here[0:1], 0.0, r1l)
-        r2l = jnp.where(here[0:1], 0.0, r2l)
-        clear = here & later
-        h = jnp.where(clear, 0.0, h)
-        l = jnp.where(clear, 0.0, l)
-        p, q = mul_pair(n1h, n1l, r1h, r1l)
-        s, t = two_sum(h, -p)
-        p2, q2 = mul_pair(n2h, n2l, r2h, r2l)
-        s, t2 = two_sum(s, -p2)
-        t = (t + t2) + (l - (q + q2))
-        h = s + t
-        l = t - (h - s)
-    mh[first:, :] = h
-    ml[first:, :] = l
+        r1 = (jnp.where(here1, 1.0, jnp.where(here2, 0.0, r1[0])), jnp.where(here, 0.0, r1[1]))
+        r2 = (jnp.where(here2, 1.0, jnp.where(here1, 0.0, r2[0])), jnp.where(here, 0.0, r2[1]))
+        m[0] = sub_pairs(*masked(jnp.logical_not(here & later), m[0]), n1, r1, n2, r2)
+        steps.append((here, w1, w2, r1, r2))
+    for t in range(1, tiles):
+        index = half + (rows + (first + 8 * t))
+
+        def spread(v):
+            return tuple(jnp.take_along_axis(part, index, axis=1) for part in v)
+
+        for here, w1, w2, r1, r2 in steps:
+            m[t] = sub_pairs(*masked(jnp.logical_not(here), m[t]), spread(w1), r1, spread(w2), r2)
+    for t in range(tiles):
+        mh[first + 8 * t : first + 8 * t + 8, :] = m[t][0]
+        ml[first + 8 * t : first + 8 * t + 8, :] = m[t][1]
 
 
 def factor_pair(mh, ml, begin, end):
@@ -384,7 +401,7 @@
         forward[d].wait_recv()
         times_pair(d)
     for m in range(mats):
-        pw[m] = jnp.transpose(pt[m])
+        pw[m] = six_right(jnp.transpose(pt[m]), 1)
 
     for d in [ny, 0] + arrivals:
         q = pairs - 1 if d == ny else y_peer(d)
@@ -392,9 +409,9 @@
         for i in range(1, nx):
             t_x[d, i].wait_recv()
             acc = acc + xrecv[d, i]
-        zsend[q] = acc.reshape(zsend.shape[1:])
-    t_z = [send(zsend.at[:, z_peer(j)], zrecv.at[j], (tz_send, tz_recv), j, (x * nz + z_peer(j), col)) for j in far_first]
-    zrecv[0] = zsend[:, z]
+        zsend[:, q] = acc.reshape(nz, *zsend.shape[2:])
+    t_z = [send(zsend.at[z_peer(j)], zrecv.at[j], (tz_send, tz_recv), j, (x * nz + z_peer(j), col)) for j in far_first]
+    zrecv[0] = zsend[z]
 
     for c in to_z:
         c.wait_recv()
@@ -408,13 +425,13 @@
     acc = zrecv[0]
     for j in range(1, nz):
         acc = acc + zrecv[j]
-    tfull[:, x, z] = acc
-    a_z = {j: send(tfull.at[:, x, z], tfull.at[:, x, z], (az_send, az_recv), j, (x * nz + z_peer(j), col))
+    tfull[x, z] = acc
+    a_z = {j: send(tfull.at[x, z], tfull.at[x, z], (az_send, az_recv), j, (x * nz + z_peer(j), col))
            for j in far_first}
     a_x = []
 
     def pass_on(j):
-        p = tfull.at[:, x, z_peer(nz - j)] if j else tfull.at[:, x, z]
+        p = tfull.at[x, z_peer(nz - j)] if j else tfull.at[x, z]
         for i in range(1, nx):
             a_x.append(send(p, p, (ax_send, ax_recv), (i, j), (x_peer(i) * nz + z, col)))
 
@@ -447,12 +464,13 @@
     pass_next(nz)
 
     def inverse_at(m):
-        return jnp.concatenate([linv[m][:, 0:RANK], linv[m][:, RANK:]], axis=0)
+        return six_left(jnp.concatenate([linv[m][:, 0:RANK], linv[m][:, RANK:]], axis=0))
 
     for c in spread + a_x:
         c.wait_recv()
-    squares = jnp.zeros((8, 128), F32)
-    places = lax.broadcasted_iota(jnp.int32, (8, 256), 0)
+    squares = jnp.zeros((16, 128), F32)
+    places = lax.broadcasted_iota(jnp.int32, (16, 256), 0)
+    inverses = [inverse_at(m) for m in range(mats)]
     for pair in range(0, mats, 2):
         sqs = []
         for m in (pair, pair + 1):
@@ -460,18 +478,19 @@
                 sqs.append(jnp.zeros((RANK, 256), F32))
                 continue
             at, to = (m % 2) * RANK // depth, (m % 2) * RANK % depth
-            t = jnp.concatenate([tfull[m // 2, h * nx // 2 + at].reshape(depth, 128)[to : to + RANK] for h in range(2)], axis=1)
-            p = nn(inverse_at(m), t, HIGHEST)
+            t = jnp.concatenate([tfull[h * nx // 2 + at, :, m // 2].reshape(depth, 128)[to : to + RANK] for h in range(2)], axis=1)
+            p = nn(inverses[m], six_right(t, 0))
             prod_out[m] = p
             sqs.append(p * p)
-        ones = jnp.where(places == pair // 2, 1.0, 0.0)
-        squares = squares + nt(ones, jnp.concatenate(sqs, axis=0), HIGHEST)
-    sq[col] = squares
+        ones = jnp.where(places == pair // 2, 1.0, 0.0).astype(BF16)
+        both = jnp.concatenate(sqs, axis=0)
+        high = both.astype(BF16)
+        squares = squares + nt(ones, high) + nt(ones, (both - high.astype(F32)).astype(BF16))
+    sq[col] = squares[0:8]
     to_all = [send(sq.at[col], sq.at[col], (sq_send, sq_recv), i, (row, lax.rem(col + i, nc))) for i in range(1, nc)]
     left = lax.broadcasted_iota(jnp.int32, (pw.shape[1], 3 * RANK), 1) < 2 * RANK
     for m in range(mats):
-        li = inverse_at(m)
-        q = nt(pw[m], jnp.concatenate([li, li, li], axis=0), HIGHEST)
+        q = nt(pw[m], jnp.concatenate([inverses[m]] * 3, axis=0))
         q1 = q.astype(BF16)
         pieces = jnp.where(left, q1.astype(F32), q - q1.astype(F32)).astype(BF16)
         q_out[m] = pieces
@@ -546,7 +565,7 @@
             pltpu.VMEM((ny, RANK + half, rows), F32),
             pltpu.VMEM((ny, RANK + half, rows), F32),
             pltpu.VMEM((mats, RANK, rows), F32),
-            pltpu.VMEM((mats, rows, RANK), F32),
+            pltpu.VMEM((mats, rows, 6 * RANK), BF16),
             pltpu.VMEM((2, RANK, 128), F32),
             pltpu.VMEM((nx, 2, share, 128), F32),
             pltpu.VMEM((nz, 2, share, 128), F32),
@@ -556,9 +575,9 @@
             pltpu.VMEM((mats, half, 128), F32),
             pltpu.VMEM((pairs, nx, block, 128), F32),
             pltpu.VMEM((pairs, nx, block, 128), F32),
-            pltpu.VMEM((pairs, nz, tile, 128), F32),
             pltpu.VMEM((nz, pairs, tile, 128), F32),
-            pltpu.VMEM((pairs, nx, nz, tile, 128), F32),
+            pltpu.VMEM((nz, pairs, tile, 128), F32),
+            pltpu.VMEM((nx, nz, pairs, tile, 128), F32),
             pltpu.VMEM((nc, 8, 128), F32),
             dma((2 * mats + 1,)),
             dma,

time: 62.5 us -> 60.6 us (0.970)
  Pallas kernels: 61.8 us -> 59.9 us
    pallas_call x1, Pallas kernels: 59.5 us -> 57.6 us  [body(): pl.pallas_call(functools.partial(exchange_kernel, nx, nz, ny), out_shape=...]
where the time goes in v5:
time: 60.6 us; the launch traced here: 60.5 us
  Pallas kernels  59.9 us (99%)
  between operations  0.64 us (1%)
    pallas_call x1, Pallas kernels, body(): pl.pallas_call(functools.partial(exchange_kernel, nx, nz, ny), out_shape=...  57.6 us
    pallas_call x1, Pallas kernels, body(): pl.pallas_call(functools.partial(update_kernel, gain), out_shape=(jax.Sha...  2.33 us

profile of v5, /device:TPU:1, one launch (start us, length us, event | category | flops | bytes accessed | tf_op | source)
XLA Modules:
  0.0 60.5 jit_solution(4000755241583020448)
XLA Ops:
  0.6 57.6 %exchange.1 = (f32[9,224,256]{2,1,0:T(8,128)S(1)}, f32[9,224,256]{2,1,0:T(8,128)S(1)}, bf16[9,224,192]{2,1,0:T(8,128)(2,1)S(1)}, f32[9,64,256]{2,1,0:T(8,128)S(1)}, f32[128,8]{1,0:T(8,128)S(1)}) custom-call(f32[9,224,256]{2,1,0:T(8,128)} %weight.1, bf16[9,224,256]{2,1,0:T(8,128)(2,1)} %grad.1, f32[9,224,256]{2,1,0:T(8,128)} %mom.1, f32[9,64,256]{2,1,0:T(8,128)} %bitcast.2), custom_call_target="tpu_custom_call" | custom-call | tf_op jit(solution)/shard_map/exchange/pallas_call | solution.py:548
  58.2 2.3 %update.1 = (f32[9,224,256]{2,1,0:T(8,128)}, f32[9,224,256]{2,1,0:T(8,128)}, f32[9,64,256]{2,1,0:T(8,128)}) custom-call(f32[9,224,256]{2,1,0:T(8,128)S(1)} %get-tuple-element.11.w, f32[9,224,256]{2,1,0:T(8,128)S(1)} %get-tuple-element.12.mom, bf16[9,224,192]{2,1,0:T(8,128)(2,1)S(1)} %get-tuple-element.13.q, f32[9,64,256]{2,1,0:T(8,128)S(1)} %get-tuple-element.14.prod, ...), custom_call_target="tpu_custom_call" | custom-call | tf_op jit(solution)/shard_map/update/pallas_call | solution.py:606

commit v6 on v5

--- a/solution.py
+++ b/solution.py
@@ -400,18 +400,28 @@
             pass_power(d)
         forward[d].wait_recv()
         times_pair(d)
+    turn_order = [ny, 0] + arrivals
+    cut_at = (len(turn_order) + 1) // 2
+    groups = [turn_order[:cut_at], turn_order[cut_at:]]
+
+    def pair_of(d):
+        return pairs - 1 if d == ny else y_peer(d)
+
+    def sum_over_x(g):
+        for n, d in enumerate(groups[g]):
+            acc = tp[pair_of(d), x]
+            for i in range(1, nx):
+                t_x[d, i].wait_recv()
+                acc = acc + xrecv[d, i]
+            zsend[g][:, n] = acc.reshape(nz, *zsend[g].shape[2:])
+        zrecv[g][0] = zsend[g][z]
+        return [send(zsend[g].at[z_peer(j)], zrecv[g].at[j], (tz_send, tz_recv), (g, j), (x * nz + z_peer(j), col))
+                for j in far_first]
+
+    t_z = [sum_over_x(0)]
     for m in range(mats):
         pw[m] = six_right(jnp.transpose(pt[m]), 1)
-
-    for d in [ny, 0] + arrivals:
-        q = pairs - 1 if d == ny else y_peer(d)
-        acc = tp[q, x]
-        for i in range(1, nx):
-            t_x[d, i].wait_recv()
-            acc = acc + xrecv[d, i]
-        zsend[:, q] = acc.reshape(nz, *zsend.shape[2:])
-    t_z = [send(zsend.at[z_peer(j)], zrecv.at[j], (tz_send, tz_recv), j, (x * nz + z_peer(j), col)) for j in far_first]
-    zrecv[0] = zsend[z]
+    t_z.append(sum_over_x(1))
 
     for c in to_z:
         c.wait_recv()
@@ -420,77 +430,84 @@
     ga[x, 1] = l
     to_a = [send(ga.at[x], ga.at[x], (ga_send, ga_recv), i, (x_peer(i) * nz + z, col)) for i in range(1, nx)]
 
-    for c in t_z:
-        c.wait_recv()
-    acc = zrecv[0]
-    for j in range(1, nz):
-        acc = acc + zrecv[j]
-    tfull[x, z] = acc
-    a_z = {j: send(tfull.at[x, z], tfull.at[x, z], (az_send, az_recv), j, (x * nz + z_peer(j), col))
-           for j in far_first}
-    a_x = []
-
-    def pass_on(j):
-        p = tfull.at[x, z_peer(nz - j)] if j else tfull.at[x, z]
+    a_z, a_x = {}, []
+
+    def pass_on(g, j):
+        if j:
+            a_z[g, j].wait_recv()
+        p = tfull[g].at[x, z_peer(nz - j)] if j else tfull[g].at[x, z]
         for i in range(1, nx):
-            a_x.append(send(p, p, (ax_send, ax_recv), (i, j), (x_peer(i) * nz + z, col)))
-
-    pass_on(0)
+            a_x.append(send(p, p, (ax_send, ax_recv), (g, i, j), (x_peer(i) * nz + z, col)))
+
+    for g in range(2):
+        for c in t_z[g]:
+            c.wait_recv()
+        acc = zrecv[g][0]
+        for j in range(1, nz):
+            acc = acc + zrecv[g][j]
+        tfull[g][x, z] = acc
+        for j in far_first:
+            a_z[g, j] = send(tfull[g].at[x, z], tfull[g].at[x, z], (az_send, az_recv), (g, j), (x * nz + z_peer(j), col))
+        pass_on(g, 0)
+
     for c in to_a:
         c.wait_recv()
     for i in range(nx):
         mh[i * share : (i + 1) * share, :] = ga[i, 0]
         ml[i * share : (i + 1) * share, :] = ga[i, 1]
     near_first = far_first[::-1]
-
-    def pass_next(n):
-        for j in near_first[:n]:
-            a_z[j].wait_recv()
-            pass_on(j)
-        del near_first[:n]
-
+    near = near_first[:4]
+    rest = near_first[4:]
     factor_pair(mh, ml, 0, 32)
-    pass_next(2)
+    for j in near:
+        pass_on(0, j)
     factor_pair(mh, ml, 32, 48)
-    pass_next(2)
+    for j in rest:
+        pass_on(0, j)
     factor_pair(mh, ml, 48, RANK)
-
     inverse = inverse_of(mh, ml)
     low = pltpu.roll(inverse[half:], 64, 1)
     first_lanes = lax.broadcasted_iota(jnp.int32, (half, 128), 1) < 64
     linv[own] = jnp.where(first_lanes, inverse[0:half], low)
     linv[last] = jnp.where(first_lanes, pltpu.roll(inverse[0:half], 64, 1), inverse[half:])
     spread = [send(linv.at[own], linv.at[own], (l_send, l_recv), i, (row, lax.rem(col + i, nc))) for i in range(1, nc)]
-    pass_next(nz)
-
-    def inverse_at(m):
-        return six_left(jnp.concatenate([linv[m][:, 0:RANK], linv[m][:, RANK:]], axis=0))
-
-    for c in spread + a_x:
+    for j in near_first:
+        pass_on(1, j)
+    for c in spread:
         c.wait_recv()
+    inverses = {}
+    for d in turn_order:
+        for e in range(1 if d == ny else 2):
+            packed = linv[2 * pair_of(d) + e]
+            inverses[d, e] = six_left(jnp.concatenate([packed[:, 0:RANK], packed[:, RANK:]], axis=0))
+    for c in a_x:
+        c.wait_recv()
+
     squares = jnp.zeros((16, 128), F32)
     places = lax.broadcasted_iota(jnp.int32, (16, 256), 0)
-    inverses = [inverse_at(m) for m in range(mats)]
-    for pair in range(0, mats, 2):
-        sqs = []
-        for m in (pair, pair + 1):
-            if m >= mats:
-                sqs.append(jnp.zeros((RANK, 256), F32))
-                continue
-            at, to = (m % 2) * RANK // depth, (m % 2) * RANK % depth
-            t = jnp.concatenate([tfull[h * nx // 2 + at, :, m // 2].reshape(depth, 128)[to : to + RANK] for h in range(2)], axis=1)
-            p = nn(inverses[m], six_right(t, 0))
-            prod_out[m] = p
-            sqs.append(p * p)
-        ones = jnp.where(places == pair // 2, 1.0, 0.0).astype(BF16)
-        both = jnp.concatenate(sqs, axis=0)
-        high = both.astype(BF16)
-        squares = squares + nt(ones, high) + nt(ones, (both - high.astype(F32)).astype(BF16))
+    for g in range(2):
+        for n, d in enumerate(groups[g]):
+            sqs = []
+            for e in range(2):
+                if (d, e) not in inverses:
+                    sqs.append(jnp.zeros((RANK, 256), F32))
+                    continue
+                at, to = e * RANK // depth, e * RANK % depth
+                t = jnp.concatenate([tfull[g][h * nx // 2 + at, :, n].reshape(depth, 128)[to : to + RANK]
+                                     for h in range(2)], axis=1)
+                p = nn(inverses[d, e], six_right(t, 0))
+                prod_out[2 * pair_of(d) + e] = p
+                sqs.append(p * p)
+            ones = jnp.where(places == pair_of(d), 1.0, 0.0).astype(BF16)
+            both = jnp.concatenate(sqs, axis=0)
+            high = both.astype(BF16)
+            squares = squares + nt(ones, high) + nt(ones, (both - high.astype(F32)).astype(BF16))
     sq[col] = squares[0:8]
     to_all = [send(sq.at[col], sq.at[col], (sq_send, sq_recv), i, (row, lax.rem(col + i, nc))) for i in range(1, nc)]
     left = lax.broadcasted_iota(jnp.int32, (pw.shape[1], 3 * RANK), 1) < 2 * RANK
-    for m in range(mats):
-        q = nt(pw[m], jnp.concatenate([inverses[m]] * 3, axis=0))
+    for d, e in inverses:
+        m = 2 * pair_of(d) + e
+        q = nt(pw[m], jnp.concatenate([inverses[d, e]] * 3, axis=0))
         q1 = q.astype(BF16)
         pieces = jnp.where(left, q1.astype(F32), q - q1.astype(F32)).astype(BF16)
         q_out[m] = pieces
@@ -538,6 +555,7 @@
     ff = cols * nc
     rt = jnp.transpose(right, (1, 2, 0))
     pairs = (mats + 1) // 2
+    sizes = ((pairs + 1) // 2, pairs // 2)
     block = 256 // nx
     tile = block // nz
     share = RANK // nx
@@ -575,9 +593,9 @@
             pltpu.VMEM((mats, half, 128), F32),
             pltpu.VMEM((pairs, nx, block, 128), F32),
             pltpu.VMEM((pairs, nx, block, 128), F32),
-            pltpu.VMEM((nz, pairs, tile, 128), F32),
-            pltpu.VMEM((nz, pairs, tile, 128), F32),
-            pltpu.VMEM((nx, nz, pairs, tile, 128), F32),
+            [pltpu.VMEM((nz, n, tile, 128), F32) for n in sizes],
+            [pltpu.VMEM((nz, n, tile, 128), F32) for n in sizes],
+            [pltpu.VMEM((nx, nz, n, tile, 128), F32) for n in sizes],
             pltpu.VMEM((nc, 8, 128), F32),
             dma((2 * mats + 1,)),
             dma,
@@ -590,9 +608,9 @@
             dma((nz,)), dma((nz,)),
             dma((nx,)), dma((nx,)),
             dma((pairs, nx)), dma((pairs, nx)),
-            dma((nz,)), dma((nz,)),
-            dma((nz,)), dma((nz,)),
-            dma((nx, nz)), dma((nx, nz)),
+            dma((2, nz)), dma((2, nz)),
+            dma((2, nz)), dma((2, nz)),
+            dma((2, nx, nz)), dma((2, nx, nz)),
             dma((nc,)), dma((nc,)),
             dma((nc,)), dma((nc,)),
         ],

time: 60.6 us -> 58.4 us (0.964)
  Pallas kernels: 59.9 us -> 57.7 us
    pallas_call x1, Pallas kernels: 57.6 us -> 55.4 us  [body(): pl.pallas_call(functools.partial(exchange_kernel, nx, nz, ny), out_shape=...]
where the time goes in v6:
time: 58.4 us; the launch traced here: 58.3 us
  Pallas kernels  57.7 us (99%)
  between operations  0.64 us (1%)
    pallas_call x1, Pallas kernels, body(): pl.pallas_call(functools.partial(exchange_kernel, nx, nz, ny), out_shape=...  55.4 us
    pallas_call x1, Pallas kernels, body(): pl.pallas_call(functools.partial(update_kernel, gain), out_shape=(jax.Sha...  2.33 us

profile of v6, /device:TPU:1, one launch (start us, length us, event | category | flops | bytes accessed | tf_op | source)
XLA Modules:
  0.0 58.3 jit_solution(7211266271253623297)
XLA Ops:
  0.6 55.4 %exchange.1 = (f32[9,224,256]{2,1,0:T(8,128)S(1)}, f32[9,224,256]{2,1,0:T(8,128)S(1)}, bf16[9,224,192]{2,1,0:T(8,128)(2,1)S(1)}, f32[9,64,256]{2,1,0:T(8,128)S(1)}, f32[128,8]{1,0:T(8,128)S(1)}) custom-call(f32[9,224,256]{2,1,0:T(8,128)} %weight.1, bf16[9,224,256]{2,1,0:T(8,128)(2,1)} %grad.1, f32[9,224,256]{2,1,0:T(8,128)} %mom.1, f32[9,64,256]{2,1,0:T(8,128)} %bitcast.2), custom_call_target="tpu_custom_call" | custom-call | tf_op jit(solution)/shard_map/exchange/pallas_call | solution.py:566
  56.0 2.3 %update.1 = (f32[9,224,256]{2,1,0:T(8,128)}, f32[9,224,256]{2,1,0:T(8,128)}, f32[9,64,256]{2,1,0:T(8,128)}) custom-call(f32[9,224,256]{2,1,0:T(8,128)S(1)} %get-tuple-element.11.w, f32[9,224,256]{2,1,0:T(8,128)S(1)} %get-tuple-element.12.mom, bf16[9,224,192]{2,1,0:T(8,128)(2,1)S(1)} %get-tuple-element.13.q, f32[9,64,256]{2,1,0:T(8,128)S(1)} %get-tuple-element.14.prod, ...), custom_call_target="tpu_custom_call" | custom-call | tf_op jit(solution)/shard_map/update/pallas_call | solution.py:624

commit v7 on v6

--- a/solution.py
+++ b/solution.py
@@ -261,6 +261,12 @@
 
     far_first = sorted(range(1, nz), key=lambda i: -min(i, nz - i))
 
+    barrier = pltpu.get_barrier_semaphore()
+    peers = [(x * nz + z_peer(i), col) for i in far_first]
+    peers += [(row, lax.rem(col + i, nc)) for i in range(1, nc)]
+    peers += [(x_peer(i) * nz + z, col) for i in range(1, nx)]
+    for peer in peers:
+        pl.semaphore_signal(barrier, inc=1, device_id=peer, device_id_type=MESH)
     load_right = pltpu.make_async_copy(right, r_v, load_sem.at[2 * mats])
     load_right.start()
 
@@ -273,12 +279,6 @@
         for c in loads(m):
             c.start()
 
-    barrier = pltpu.get_barrier_semaphore()
-    peers = [(row, lax.rem(col + i, nc)) for i in range(1, nc)]
-    peers += [(x * nz + z_peer(i), col) for i in far_first]
-    peers += [(x_peer(i) * nz + z, col) for i in range(1, nx)]
-    for peer in peers:
-        pl.semaphore_signal(barrier, inc=1, device_id=peer, device_id_type=MESH)
     load_right.wait()
 
     def power(m):
@@ -380,8 +380,10 @@
     block_out(ny, pairs - 1)
     forward[0].wait_recv()
     times_pair(0)
-    for d in arrivals[:-1]:
+    for d in arrivals:
         pass_power(d)
+    forward[arrivals[0]].wait_recv()
+    times_pair(arrivals[0])
 
     def sum_pairs(ref, n):
         h, l = ref[0, 0], ref[0, 1]
@@ -395,9 +397,7 @@
     gz[z, 0] = h
     gz[z, 1] = l
     to_z = [send(gz.at[z], gz.at[z], (gz_send, gz_recv), i, (x * nz + z_peer(i), col)) for i in far_first]
-    for n, d in enumerate(arrivals):
-        if n == ny - 2:
-            pass_power(d)
+    for d in arrivals[1:]:
         forward[d].wait_recv()
         times_pair(d)
     turn_order = [ny, 0] + arrivals
@@ -430,14 +430,14 @@
     ga[x, 1] = l
     to_a = [send(ga.at[x], ga.at[x], (ga_send, ga_recv), i, (x_peer(i) * nz + z, col)) for i in range(1, nx)]
 
-    a_z, a_x = {}, []
+    a_z, a_x = {}, ([], [])
 
     def pass_on(g, j):
         if j:
             a_z[g, j].wait_recv()
         p = tfull[g].at[x, z_peer(nz - j)] if j else tfull[g].at[x, z]
         for i in range(1, nx):
-            a_x.append(send(p, p, (ax_send, ax_recv), (g, i, j), (x_peer(i) * nz + z, col)))
+            a_x[g].append(send(p, p, (ax_send, ax_recv), (g, i, j), (x_peer(i) * nz + z, col)))
 
     for g in range(2):
         for c in t_z[g]:
@@ -480,12 +480,11 @@
         for e in range(1 if d == ny else 2):
             packed = linv[2 * pair_of(d) + e]
             inverses[d, e] = six_left(jnp.concatenate([packed[:, 0:RANK], packed[:, RANK:]], axis=0))
-    for c in a_x:
-        c.wait_recv()
-
     squares = jnp.zeros((16, 128), F32)
     places = lax.broadcasted_iota(jnp.int32, (16, 256), 0)
     for g in range(2):
+        for c in a_x[g]:
+            c.wait_recv()
         for n, d in enumerate(groups[g]):
             sqs = []
             for e in range(2):

time: 58.4 us -> 58.1 us (level)
  no operation moved by 1% of the time
where the time goes in v7:
time: 58.1 us; the launch traced here: 58 us
  Pallas kernels  57.4 us (99%)
  between operations  0.64 us (1%)
    pallas_call x1, Pallas kernels, body(): pl.pallas_call(functools.partial(exchange_kernel, nx, nz, ny), out_shape=...  55 us
    pallas_call x1, Pallas kernels, body(): pl.pallas_call(functools.partial(update_kernel, gain), out_shape=(jax.Sha...  2.33 us

profile of v7, /device:TPU:1, one launch (start us, length us, event | category | flops | bytes accessed | tf_op | source)
XLA Modules:
  0.0 58.0 jit_solution(3596435703797056723)
XLA Ops:
  0.6 55.0 %exchange.1 = (f32[9,224,256]{2,1,0:T(8,128)S(1)}, f32[9,224,256]{2,1,0:T(8,128)S(1)}, bf16[9,224,192]{2,1,0:T(8,128)(2,1)S(1)}, f32[9,64,256]{2,1,0:T(8,128)S(1)}, f32[128,8]{1,0:T(8,128)S(1)}) custom-call(f32[9,224,256]{2,1,0:T(8,128)} %weight.1, bf16[9,224,256]{2,1,0:T(8,128)(2,1)} %grad.1, f32[9,224,256]{2,1,0:T(8,128)} %mom.1, f32[9,64,256]{2,1,0:T(8,128)} %bitcast.2), custom_call_target="tpu_custom_call" | custom-call | tf_op jit(solution)/shard_map/exchange/pallas_call | solution.py:565
  55.7 2.3 %update.1 = (f32[9,224,256]{2,1,0:T(8,128)}, f32[9,224,256]{2,1,0:T(8,128)}, f32[9,64,256]{2,1,0:T(8,128)}) custom-call(f32[9,224,256]{2,1,0:T(8,128)S(1)} %get-tuple-element.11.w, f32[9,224,256]{2,1,0:T(8,128)S(1)} %get-tuple-element.12.mom, bf16[9,224,192]{2,1,0:T(8,128)(2,1)S(1)} %get-tuple-element.13.q, f32[9,64,256]{2,1,0:T(8,128)S(1)} %get-tuple-element.14.prod, ...), custom_call_target="tpu_custom_call" | custom-call | tf_op jit(solution)/shard_map/update/pallas_call | solution.py:623

commit v8 on v7

--- a/solution.py
+++ b/solution.py
@@ -226,7 +226,7 @@
                     mate, ysend, yrecv, pt, pw, gp, gx, gz, ga, mh, ml, linv, tp, xrecv, zsend, zrecv, tfull, sq, load_sem,
                     w_sem, mate_send, mate_recv, y_send, y_recv, ag_send, ag_recv, fw_send, fw_recv, h_send, h_recv,
                     gx_send, gx_recv, gz_send, gz_recv, ga_send, ga_recv, tx_send, tx_recv, tz_send, tz_recv, az_send,
-                    az_recv, ax_send, ax_recv, l_send, l_recv, sq_send, sq_recv):
+                    az_recv, ax_send, ax_recv, l_send, l_recv, sq_send, sq_recv, near_sem, far_sem):
     nr, nc = nx * nz, ny * 2
     mats = nc + 1
     last = mats - 1
@@ -262,9 +262,10 @@
     far_first = sorted(range(1, nz), key=lambda i: -min(i, nz - i))
 
     barrier = pltpu.get_barrier_semaphore()
-    peers = [(x * nz + z_peer(i), col) for i in far_first]
-    peers += [(row, lax.rem(col + i, nc)) for i in range(1, nc)]
-    peers += [(x_peer(i) * nz + z, col) for i in range(1, nx)]
+    along_z = [(x * nz + z_peer(i), col) for i in (1, nz - 1)]
+    along_x = [(x_peer(i) * nz + z, col) for i in (1, nx - 1)]
+    two_off = [(x * nz + z_peer(i), col) for i in (2, nz - 2)]
+    peers = along_z + along_x + [(row, lax.rem(col + i, nc)) for i in range(1, nc)]
     for peer in peers:
         pl.semaphore_signal(barrier, inc=1, device_id=peer, device_id_type=MESH)
     load_right = pltpu.make_async_copy(right, r_v, load_sem.at[2 * mats])
@@ -300,6 +301,8 @@
     other_rows = pl.ds(pl.multiple_of((1 - k) * half, half), half)
     my_rows = pl.ds(pl.multiple_of(k * half, half), half)
     to_mate[ny] = send(part.at[last, other_rows], mate.at[ny, pl.ds(0, half)], mate_sems, ny, mate_id)
+    for peer in along_z + along_x:
+        pl.semaphore_signal(near_sem, inc=1, device_id=peer, device_id_type=MESH)
     load_weight = pltpu.make_async_copy(weight, w_out, w_sem)
     load_weight.start()
 
@@ -319,6 +322,9 @@
             ysend[i, 0:RANK, :] = part[2 * yd + k] + mate[i]
             ysend[i, RANK:, :] = shared
             to_y.append(send(ysend.at[i], yrecv.at[y], (y_send, y_recv), i, (row, 2 * yd + k)))
+    pl.semaphore_wait(near_sem, len(along_z + along_x))
+    for peer in two_off:
+        pl.semaphore_signal(far_sem, inc=1, device_id=peer, device_id_type=MESH)
     for c in to_y:
         c.wait_recv()
     total = yrecv[0]
@@ -345,6 +351,7 @@
             for i in range(1, nx)]
     gx[x] = gp[:, rows_of(x), :]
 
+    pl.semaphore_wait(far_sem, len(two_off))
     pairs = tp.shape[0]
     depth = tp.shape[2]
     t_x = {}
@@ -612,6 +619,8 @@
             dma((2, nx, nz)), dma((2, nx, nz)),
             dma((nc,)), dma((nc,)),
             dma((nc,)), dma((nc,)),
+            pltpu.SemaphoreType.REGULAR,
+            pltpu.SemaphoreType.REGULAR,
         ],
         compiler_params=pltpu.CompilerParams(
             collective_id=0, has_side_effects=True, vmem_limit_bytes=40 * 1024 * 1024

time: 58.1 us -> 58.1 us (level)
  no operation moved by 1% of the time
where the time goes in v8:
time: 58.1 us; the launch traced here: 58 us
  Pallas kernels  57.3 us (99%)
  between operations  0.64 us (1%)
    pallas_call x1, Pallas kernels, body(): pl.pallas_call(functools.partial(exchange_kernel, nx, nz, ny), out_shape=...  55 us
    pallas_call x1, Pallas kernels, body(): pl.pallas_call(functools.partial(update_kernel, gain), out_shape=(jax.Sha...  2.33 us

profile of v8, /device:TPU:1, one launch (start us, length us, event | category | flops | bytes accessed | tf_op | source)
XLA Modules:
  0.0 58.0 jit_solution(5495027852698826659)
XLA Ops:
  0.6 55.0 %exchange.1 = (f32[9,224,256]{2,1,0:T(8,128)S(1)}, f32[9,224,256]{2,1,0:T(8,128)S(1)}, bf16[9,224,192]{2,1,0:T(8,128)(2,1)S(1)}, f32[9,64,256]{2,1,0:T(8,128)S(1)}, f32[128,8]{1,0:T(8,128)S(1)}) custom-call(f32[9,224,256]{2,1,0:T(8,128)} %weight.1, bf16[9,224,256]{2,1,0:T(8,128)(2,1)} %grad.1, f32[9,224,256]{2,1,0:T(8,128)} %mom.1, f32[9,64,256]{2,1,0:T(8,128)} %bitcast.2), custom_call_target="tpu_custom_call" | custom-call | tf_op jit(solution)/shard_map/exchange/pallas_call | solution.py:572
  55.7 2.3 %update.1 = (f32[9,224,256]{2,1,0:T(8,128)}, f32[9,224,256]{2,1,0:T(8,128)}, f32[9,64,256]{2,1,0:T(8,128)}) custom-call(f32[9,224,256]{2,1,0:T(8,128)S(1)} %get-tuple-element.11.w, f32[9,224,256]{2,1,0:T(8,128)S(1)} %get-tuple-element.12.mom, bf16[9,224,192]{2,1,0:T(8,128)(2,1)S(1)} %get-tuple-element.13.q, f32[9,64,256]{2,1,0:T(8,128)S(1)} %get-tuple-element.14.prod, ...), custom_call_target="tpu_custom_call" | custom-call | tf_op jit(solution)/shard_map/update/pallas_call | solution.py:632

commit v9 on v8

--- a/solution.py
+++ b/solution.py
@@ -268,19 +268,17 @@
     peers = along_z + along_x + [(row, lax.rem(col + i, nc)) for i in range(1, nc)]
     for peer in peers:
         pl.semaphore_signal(barrier, inc=1, device_id=peer, device_id_type=MESH)
-    load_right = pltpu.make_async_copy(right, r_v, load_sem.at[2 * mats])
-    load_right.start()
-
     def loads(m):
         return (pltpu.make_async_copy(mom.at[m], s_v.at[m], load_sem.at[m]),
-                pltpu.make_async_copy(grad.at[m], g_v.at[m], load_sem.at[mats + m]))
-
-    turns = list(range(1, ny)) + [0]
+                pltpu.make_async_copy(grad.at[m], g_v.at[m], load_sem.at[mats + m]),
+                pltpu.make_async_copy(right.at[m], r_v.at[m], load_sem.at[2 * mats + m]))
+
+    far_y = sorted(range(1, ny), key=lambda i: -min(i, ny - i))
+    turns = far_y + [0]
     for m in [2 * y_peer(i) + (1 - k) for i in turns] + [last] + [2 * y_peer(i) + k for i in turns]:
         for c in loads(m):
             c.start()
 
-    load_right.wait()
 
     def power(m):
         for c in loads(m):
@@ -333,7 +331,7 @@
     pt[last, my_rows, :] = total[RANK:]
     swap = send(pt.at[last, my_rows], pt.at[last, my_rows], (h_send, h_recv), 0, mate_id)
     pt[own] = total[0:RANK]
-    gather = [send(pt.at[own], pt.at[own], (ag_send, ag_recv), i, (row, 2 * y_peer(i) + k)) for i in range(1, ny)]
+    gather = {i: send(pt.at[own], pt.at[own], (ag_send, ag_recv), i, (row, 2 * y_peer(i) + k)) for i in far_y}
     forward = {0: send(pt.at[own], pt.at[own], (fw_send, fw_recv), 0, mate_id)}
 
     lanes = lax.broadcasted_iota(jnp.int32, (RANK, 128), 1)
@@ -376,7 +374,7 @@
     arrivals = sorted(range(1, ny), key=lambda d: min(d, ny - d))
 
     def pass_power(d):
-        gather[ny - d - 1].wait_recv()
+        gather[ny - d].wait_recv()
         m = 2 * y_peer(d) + k
         forward[d] = send(pt.at[m], pt.at[m], (fw_send, fw_recv), d, mate_id)
 
@@ -426,8 +424,6 @@
                 for j in far_first]
 
     t_z = [sum_over_x(0)]
-    for m in range(mats):
-        pw[m] = six_right(jnp.transpose(pt[m]), 1)
     t_z.append(sum_over_x(1))
 
     for c in to_z:
@@ -437,6 +433,8 @@
     ga[x, 1] = l
     to_a = [send(ga.at[x], ga.at[x], (ga_send, ga_recv), i, (x_peer(i) * nz + z, col)) for i in range(1, nx)]
 
+    for m in range(mats):
+        pw[m] = six_right(jnp.transpose(pt[m]), 1)
     a_z, a_x = {}, ([], [])
 
     def pass_on(g, j):
@@ -536,10 +534,10 @@
 
 def update_kernel(gain, w, mom, q, prod, scale, new_weight, new_mom, new_right, w_v, r_v, w_sem, m_sem, r_sem):
     mats = w.shape[0]
-    move = pltpu.make_async_copy(mom, new_mom, m_sem)
-    move.start()
+    moves = [pltpu.make_async_copy(mom.at[m], new_mom.at[m], m_sem.at[m]) for m in range(mats)]
+    for c in moves:
+        c.start()
     table = scale[...]
-    moves = [move]
     for m in range(mats):
         column = table[(m % 2) * RANK : (m % 2 + 1) * RANK, m // 2 : m // 2 + 1]
         normed = prod[m] * column
@@ -603,7 +601,7 @@
             [pltpu.VMEM((nz, n, tile, 128), F32) for n in sizes],
             [pltpu.VMEM((nx, nz, n, tile, 128), F32) for n in sizes],
             pltpu.VMEM((nc, 8, 128), F32),
-            dma((2 * mats + 1,)),
+            dma((3 * mats,)),
             dma,
             dma((ny + 1,)), dma((ny + 1,)),
             dma((ny,)), dma((ny,)),
@@ -642,7 +640,7 @@
             pltpu.VMEM((mats, rows, cols), F32),
             pltpu.VMEM((mats, RANK, cols), F32),
             dma((mats,)),
-            dma,
+            dma((mats,)),
             dma((mats,)),
         ],
         compiler_params=pltpu.CompilerParams(vmem_limit_bytes=12 * 1024 * 1024),

time: 58.1 us -> 58.2 us (level)
  no operation moved by 1% of the time
where the time goes in v9:
time: 58.2 us
  Pallas kernels  57.5 us (99%)
  between operations  0.64 us (1%)
    pallas_call x1, Pallas kernels, body(): pl.pallas_call(functools.partial(exchange_kernel, nx, nz, ny), out_shape=...  55.1 us
    pallas_call x1, Pallas kernels, body(): pl.pallas_call(functools.partial(update_kernel, gain), out_shape=(jax.Sha...  2.41 us

profile of v9, /device:TPU:1, one launch (start us, length us, event | category | flops | bytes accessed | tf_op | source)
XLA Modules:
  0.0 58.2 jit_solution(7587273620186017651)
XLA Ops:
  0.6 55.1 %exchange.1 = (f32[9,224,256]{2,1,0:T(8,128)S(1)}, f32[9,224,256]{2,1,0:T(8,128)S(1)}, bf16[9,224,192]{2,1,0:T(8,128)(2,1)S(1)}, f32[9,64,256]{2,1,0:T(8,128)S(1)}, f32[128,8]{1,0:T(8,128)S(1)}) custom-call(f32[9,224,256]{2,1,0:T(8,128)} %weight.1, bf16[9,224,256]{2,1,0:T(8,128)(2,1)} %grad.1, f32[9,224,256]{2,1,0:T(8,128)} %mom.1, f32[9,64,256]{2,1,0:T(8,128)} %bitcast.2), custom_call_target="tpu_custom_call" | custom-call | tf_op jit(solution)/shard_map/exchange/pallas_call | solution.py:570
  55.7 2.4 %update.1 = (f32[9,224,256]{2,1,0:T(8,128)}, f32[9,224,256]{2,1,0:T(8,128)}, f32[9,64,256]{2,1,0:T(8,128)}) custom-call(f32[9,224,256]{2,1,0:T(8,128)S(1)} %get-tuple-element.11.w, f32[9,224,256]{2,1,0:T(8,128)S(1)} %get-tuple-element.12.mom, bf16[9,224,192]{2,1,0:T(8,128)(2,1)S(1)} %get-tuple-element.13.q, f32[9,64,256]{2,1,0:T(8,128)S(1)} %get-tuple-element.14.prod, ...), custom_call_target="tpu_custom_call" | custom-call | tf_op jit(solution)/shard_map/update/pallas_call | solution.py:630

commit v10 on v8

--- a/solution.py
+++ b/solution.py
@@ -358,9 +358,9 @@
 
     def times(m, q, e):
         t = cut_product(nn, pt[m], s_v[m])
-        at, to = e * RANK // depth, e * RANK % depth
+        at, to = (e, 0) if depth == RANK else (0, e * RANK)
         for h in range(2):
-            tp[q, h * nx // 2 + at, to : to + RANK, :] = t[:, h * 128 : (h + 1) * 128]
+            tp[q, h * nx // 2 + at, pl.ds(to, RANK), :] = t[:, h * 128 : (h + 1) * 128]
 
     def block_out(turn, q):
         for i in range(1, nx):
@@ -369,8 +369,9 @@
 
     def times_pair(d):
         q = y_peer(d)
-        times(2 * q, q, 0)
-        times(2 * q + 1, q, 1)
+        times(2 * q + k, q, k)
+        forward[d].wait_recv()
+        times(2 * q + (1 - k), q, 1 - k)
         block_out(d, q)
 
     arrivals = sorted(range(1, ny), key=lambda d: min(d, ny - d))
@@ -385,11 +386,9 @@
         tp[pairs - 1, h * nx // 2 + at, to : to + RANK, :] = jnp.zeros((RANK, 128), F32)
     times(last, pairs - 1, 0)
     block_out(ny, pairs - 1)
-    forward[0].wait_recv()
     times_pair(0)
     for d in arrivals:
         pass_power(d)
-    forward[arrivals[0]].wait_recv()
     times_pair(arrivals[0])
 
     def sum_pairs(ref, n):
@@ -405,7 +404,6 @@
     gz[z, 1] = l
     to_z = [send(gz.at[z], gz.at[z], (gz_send, gz_recv), i, (x * nz + z_peer(i), col)) for i in far_first]
     for d in arrivals[1:]:
-        forward[d].wait_recv()
         times_pair(d)
     turn_order = [ny, 0] + arrivals
     cut_at = (len(turn_order) + 1) // 2
@@ -426,8 +424,6 @@
                 for j in far_first]
 
     t_z = [sum_over_x(0)]
-    for m in range(mats):
-        pw[m] = six_right(jnp.transpose(pt[m]), 1)
     t_z.append(sum_over_x(1))
 
     for c in to_z:
@@ -437,6 +433,8 @@
     ga[x, 1] = l
     to_a = [send(ga.at[x], ga.at[x], (ga_send, ga_recv), i, (x_peer(i) * nz + z, col)) for i in range(1, nx)]
 
+    for m in range(mats):
+        pw[m] = six_right(jnp.transpose(pt[m]), 1)
     a_z, a_x = {}, ([], [])
 
     def pass_on(g, j):

time: 58.1 us -> 58.1 us (level)
  no operation moved by 1% of the time
where the time goes in v10:
time: 58.1 us; the launch traced here: 58 us
  Pallas kernels  57.4 us (99%)
  between operations  0.64 us (1%)
    pallas_call x1, Pallas kernels, body(): pl.pallas_call(functools.partial(exchange_kernel, nx, nz, ny), out_shape=...  55.1 us
    pallas_call x1, Pallas kernels, body(): pl.pallas_call(functools.partial(update_kernel, gain), out_shape=(jax.Sha...  2.33 us

profile of v10, /device:TPU:1, one launch (start us, length us, event | category | flops | bytes accessed | tf_op | source)
XLA Modules:
  0.0 58.0 jit_solution(6881058797289503015)
XLA Ops:
  0.6 55.1 %exchange.1 = (f32[9,224,256]{2,1,0:T(8,128)S(1)}, f32[9,224,256]{2,1,0:T(8,128)S(1)}, bf16[9,224,192]{2,1,0:T(8,128)(2,1)S(1)}, f32[9,64,256]{2,1,0:T(8,128)S(1)}, f32[128,8]{1,0:T(8,128)S(1)}) custom-call(f32[9,224,256]{2,1,0:T(8,128)} %weight.1, bf16[9,224,256]{2,1,0:T(8,128)(2,1)} %grad.1, f32[9,224,256]{2,1,0:T(8,128)} %mom.1, f32[9,64,256]{2,1,0:T(8,128)} %bitcast.2), custom_call_target="tpu_custom_call" | custom-call | tf_op jit(solution)/shard_map/exchange/pallas_call | solution.py:570
  55.7 2.3 %update.1 = (f32[9,224,256]{2,1,0:T(8,128)}, f32[9,224,256]{2,1,0:T(8,128)}, f32[9,64,256]{2,1,0:T(8,128)}) custom-call(f32[9,224,256]{2,1,0:T(8,128)S(1)} %get-tuple-element.11.w, f32[9,224,256]{2,1,0:T(8,128)S(1)} %get-tuple-element.12.mom, bf16[9,224,192]{2,1,0:T(8,128)(2,1)S(1)} %get-tuple-element.13.q, f32[9,64,256]{2,1,0:T(8,128)S(1)} %get-tuple-element.14.prod, ...), custom_call_target="tpu_custom_call" | custom-call | tf_op jit(solution)/shard_map/update/pallas_call | solution.py:630

commit v11 on v10

--- a/solution.py
+++ b/solution.py
@@ -424,6 +424,8 @@
                 for j in far_first]
 
     t_z = [sum_over_x(0)]
+    for m in range(mats):
+        pw[m] = six_right(jnp.transpose(pt[m]), 1)
     t_z.append(sum_over_x(1))
 
     for c in to_z:
@@ -433,8 +435,6 @@
     ga[x, 1] = l
     to_a = [send(ga.at[x], ga.at[x], (ga_send, ga_recv), i, (x_peer(i) * nz + z, col)) for i in range(1, nx)]
 
-    for m in range(mats):
-        pw[m] = six_right(jnp.transpose(pt[m]), 1)
     a_z, a_x = {}, ([], [])
 
     def pass_on(g, j):

time: 58.1 us -> 58 us (level)
  no operation moved by 1% of the time
where the time goes in v11:
time: 58 us
  Pallas kernels  57.3 us (99%)
  between operations  0.64 us (1%)
    pallas_call x1, Pallas kernels, body(): pl.pallas_call(functools.partial(exchange_kernel, nx, nz, ny), out_shape=...  55 us
    pallas_call x1, Pallas kernels, body(): pl.pallas_call(functools.partial(update_kernel, gain), out_shape=(jax.Sha...  2.33 us

profile of v11, /device:TPU:1, one launch (start us, length us, event | category | flops | bytes accessed | tf_op | source)
XLA Modules:
  0.0 58.0 jit_solution(13712474751517585010)
XLA Ops:
  0.6 55.0 %exchange.1 = (f32[9,224,256]{2,1,0:T(8,128)S(1)}, f32[9,224,256]{2,1,0:T(8,128)S(1)}, bf16[9,224,192]{2,1,0:T(8,128)(2,1)S(1)}, f32[9,64,256]{2,1,0:T(8,128)S(1)}, f32[128,8]{1,0:T(8,128)S(1)}) custom-call(f32[9,224,256]{2,1,0:T(8,128)} %weight.1, bf16[9,224,256]{2,1,0:T(8,128)(2,1)} %grad.1, f32[9,224,256]{2,1,0:T(8,128)} %mom.1, f32[9,64,256]{2,1,0:T(8,128)} %bitcast.2), custom_call_target="tpu_custom_call" | custom-call | tf_op jit(solution)/shard_map/exchange/pallas_call | solution.py:570
  55.6 2.3 %update.1 = (f32[9,224,256]{2,1,0:T(8,128)}, f32[9,224,256]{2,1,0:T(8,128)}, f32[9,64,256]{2,1,0:T(8,128)}) custom-call(f32[9,224,256]{2,1,0:T(8,128)S(1)} %get-tuple-element.11.w, f32[9,224,256]{2,1,0:T(8,128)S(1)} %get-tuple-element.12.mom, bf16[9,224,192]{2,1,0:T(8,128)(2,1)S(1)} %get-tuple-element.13.q, f32[9,64,256]{2,1,0:T(8,128)S(1)} %get-tuple-element.14.prod, ...), custom_call_target="tpu_custom_call" | custom-call | tf_op jit(solution)/shard_map/update/pallas_call | solution.py:630
